TPU v7x, 512 devices: a whole 4x8x8 slice. The times are simulated.
512 devices in a mesh: dp: 16 (over z, core), pp: 16 (over x_hi, y), tp: 2 (over x_lo).
Axes of the slice: x: 4 (x_hi: 2, x_lo: 2; x = x_hi * 2 + x_lo), y: 8, z: 8, core: 2. Of those that a mesh axis runs over, the one named last changes fastest.
Arguments:
- activations: bfloat16 [16, 4096, 4096], P('pp', 'dp', 'tp'), may hold values from -6 to 6
- key_grads: bfloat16 [16, 4096, 512], P('pp', 'dp', 'tp'), may hold values from -6 to 6
- key_weight: bfloat16 [16, 4096, 512], P('pp', 'dp', 'tp'), may hold values from -0.25 to 0.25
- error_buf: bfloat16 [16, 16, 4096, 512], P('pp', 'dp', None, 'tp'), may hold values from -96 to 96
- q_prev: float32 [16, 512, 64], P('pp', 'tp'), may hold values from -0.25 to 0.25
Outputs:
- grad_prev: bfloat16 [16, 4096, 4096], P('pp', 'dp', 'tp')
- q_new: float32 [16, 512, 64], P('pp', 'tp')
All inputs are finite; a program needn't handle non-finite values.
Results may differ from a plain program's by a relative error of at most 0.015.
Values may be sent and summed in bfloat16 or wider, within the bound.
No kernel may reach another device: no remote copies, remote signals or barrier semaphores. Data moves between devices by JAX's collectives and lax.ppermute only.
A program may use at most 64 MiB of HBM per device.

v0:
```python
import jax
import jax.numpy as jnp
from jax import lax
from jax.sharding import PartitionSpec as P

HIGHEST = lax.Precision.HIGHEST


def from_behind(block, axis, distance):
    devices = range(lax.axis_size(axis))
    route = [(i - distance, i) for i in devices if i - distance in devices]
    return lax.ppermute(block, axis, route)


def orthonormal(factor, gram_matrix):
    lower_factor = jnp.linalg.cholesky(gram_matrix)
    return jax.scipy.linalg.solve_triangular(lower_factor, factor.T, lower=True).T


def on_device(activations, key_grads, key_weight, error_buf, q_prev):
    inputs_local = activations[0]
    grads_local = key_grads[0]
    weight_local = key_weight[0]
    error_local = error_buf[0, 0]
    coeffs_prev = q_prev[0]
    groups = lax.axis_size("dp")
    partial_grad = jnp.dot(
        grads_local,
        lax.all_gather(weight_local, "dp", axis=0, tiled=True).T,
        preferred_element_type=jnp.float32,
    )
    input_grad = lax.psum_scatter(
        partial_grad.astype(jnp.bfloat16), "tp", scatter_dimension=1, tiled=True
    )
    grad_prev = from_behind(input_grad, "pp", -1)
    error_float = error_local.astype(jnp.float32)
    inputs_whole = lax.all_gather(inputs_local, "tp", axis=1, tiled=True)
    summed = (
        lax.dot_general(
            inputs_whole, grads_local, (((0,), (0,)), ((), ())), preferred_element_type=jnp.float32
        )
        + error_float
    )
    factor = jnp.dot(summed, coeffs_prev, precision=HIGHEST)
    factor_rows = (
        lax.psum_scatter(factor.astype(jnp.bfloat16), "dp", scatter_dimension=0, tiled=True).astype(
            jnp.float32
        )
        / groups
    )
    gram_matrix = lax.psum(jnp.dot(factor_rows.T, factor_rows, precision=HIGHEST), "dp")
    basis = lax.all_gather(
        orthonormal(factor_rows, gram_matrix).astype(jnp.bfloat16), "dp", axis=0, tiled=True
    ).astype(jnp.float32)
    coeffs_local = lax.dot_general(
        summed,
        basis,
        (((0,), (0,)), ((), ())),
        precision=HIGHEST,
        preferred_element_type=jnp.float32,
    )
    coeffs_new = lax.psum(coeffs_local.astype(jnp.bfloat16), "dp").astype(jnp.float32) / groups
    return (grad_prev[None], coeffs_new[None])


def solution(mesh):
    return jax.shard_map(
        on_device,
        mesh=mesh,
        in_specs=(
            P("pp", "dp", "tp"),
            P("pp", "dp", "tp"),
            P("pp", "dp", "tp"),
            P("pp", "dp", None, "tp"),
            P("pp", "tp", None),
        ),
        out_specs=(P("pp", "dp", "tp"), P("pp", "tp", None)),
        check_vma=False,
    )
```

profile of v0, /device:TPU:7, one launch (start us, length us, event | category | flops | bytes accessed | tf_op | source)
XLA Modules:
  0.0 304.8 jit_solution(8592520682581562872)
XLA Ops:
  7.2 0.0 copy-start
  7.2 0.0 all-gather.7.cloned.1.call-start
  7.2 0.7 all-gather.7.cloned.1.call-update
  7.9 0.0 all-gather.5.cloned.1.call-start
  8.0 0.7 all-gather.5.cloned.1.call-update
  8.7 0.0 reduce-scatter.5.cloned.1.call-start
  8.7 46.4 %all-gather.7.cloned.1.call-done = bf16[1,256,4096]{2,1,0:T(8,128)(2,1)} async-done(((bf16[1,256,2048]{2,1,0:T(8,128)(2,1)}), bf16[1,256,4096]{2,1,0:T(8,128)(2,1)}) %all-gather.7.cloned.1.call-update) | async-done | bytes 2097168 | tf_op jit(solution)/shard_map/all_gather | solution.py:37
  55.1 3.0 convolution_add_fusion
  58.1 1.9 copy-done.1
  60.0 5.0 %convolution_convert_fusion.1 = bf16[4096,64]{0,1:T(8,128)(2,1)} fusion(f32[4096,256]{1,0:T(8,128)S(1)} %convolution_add_fusion, f32[1,256,64]{1,2,0:T(8,128)S(1)} %copy-done.2), kind=kOutput, calls=%fused_computation.2 | convolution fusion | flops 805568512 | bytes 4784128 | tf_op jit(solution)/shard_map/dot_general | solution.py:44
  65.0 0.0 reduce-scatter.5.cloned.1.call-update
  65.0 0.0 reduce-scatter.3.cloned.1.call-start
  65.1 37.4 %all-gather.5.cloned.1.call-done = bf16[1,4096,256]{2,1,0:T(8,128)(2,1)} async-done(((bf16[1,256,256]{2,1,0:T(8,128)(2,1)}), bf16[1,4096,256]{2,1,0:T(8,128)(2,1)}) %all-gather.5.cloned.1.call-update) | async-done | bytes 2097168 | tf_op jit(solution)/shard_map/all_gather | solution.py:29
  102.5 3.7 %convolution_convert_fusion = bf16[256,4096]{1,0:T(8,128)(2,1)} fusion(bf16[1,4096,256]{2,1,0:T(8,128)(2,1)} %all-gather.5.cloned.1.call-done, bf16[1,256,256]{2,1,0:T(8,128)(2,1)S(1)} %copy-done), kind=kOutput, calls=%fused_computation.1 | convolution fusion | flops 537919488 | bytes 4325376 | tf_op jit(solution)/shard_map/dot_general | solution.py:27
  106.2 0.0 reduce-scatter.3.cloned.1.call-update
  106.2 54.5 %reduce-scatter.5.cloned.1.call-done = bf16[256,64]{0,1:T(8,128)(2,1)} async-done(((bf16[4096,64]{0,1:T(8,128)(2,1)}), bf16[256,64]{0,1:T(8,128)(2,1)}) %reduce-scatter.5.cloned.1.call-update) | async-done | bytes 32784 | tf_op jit(solution)/shard_map/reduce_scatter | solution.py:46
  160.7 1.0 fusion.5
  161.7 45.7 %psum.14 = f32[64,64]{0,1:T(8,128)S(1)} all-reduce(f32[64,64]{0,1:T(8,128)S(1)} %fusion.5), channel_id=1, replica_groups=mesh['dp'=16,'pp'=16,'tp'=2] {'dp'}, use_global_device_ids=true, to_apply=%region_2.0 | all-reduce | flops 4096 | bytes 32768 | tf_op jit(solution)/shard_map/psum | solution.py:51
  207.4 0.1 copy.8
  207.5 5.8 %cholesky.16 = f32[64,64]{1,0:T(8,128)S(1)} custom-call(f32[64,64]{1,0:T(8,128)S(1)} %fusion.8), custom_call_target="Cholesky" | custom-call | tf_op jit(solution)/shard_map/jit(cholesky)/cholesky | solution.py:16
  213.4 0.6 compare_reduce_fusion
  214.0 0.7 fusion.6
  214.7 4.9 %custom-call.7 = f32[1,64,64]{1,2,0:T(8,128)S(1)} custom-call(f32[1,64,64]{2,1,0:T(8,128)S(1)} %fusion.6), custom_call_target="InvertDiagBlocksLowerTriangular" | custom-call | tf_op jit(solution)/shard_map/jit(_solve_triangular)/triangular_solve | solution.py:17
  219.6 0.0 reduce-scatter.3.cloned.1.call-done
  219.6 5.3 %collective-permute-start = (bf16[256,2048]{1,0:T(8,128)(2,1)}, bf16[256,2048]{1,0:T(8,128)(2,1)S(1)}, u32[]{:S(2)}, u32[]{:S(2)}) collective-permute-start(bf16[256,2048]{1,0:T(8,128)(2,1)} %reduce-scatter.3.cloned.1.call-done), channel_id=1, source_target_pairs={{2,0},{4,2},{6,4},{8,6},{10,8},{12,10},{14,12},{16,14},{18,16},{20... | collective-permute-start | bytes 3145736 | tf_op jit(solution)/shard_map/ppermute | solution.py:12
  225.0 1.1 convolution_convert_fusion.2
  226.1 22.0 %all_gather.11 = bf16[4096,64]{1,0:T(8,128)(2,1)S(1)} all-gather(bf16[256,64]{1,0:T(8,128)(2,1)S(1)} %convolution_convert_fusion.2), channel_id=1, replica_groups=mesh['dp'=16,'pp'=16,'tp'=2] {'dp'}, dimensions={0}, use_global_device_ids=true | all-gather | bytes 557056 | tf_op jit(solution)/shard_map/all_gather | solution.py:52
  248.1 4.0 %convolution_convert_fusion.3 = bf16[256,64]{0,1:T(8,128)(2,1)S(1)} fusion(f32[4096,256]{1,0:T(8,128)} %copy-done.1, bf16[4096,64]{1,0:T(8,128)(2,1)S(1)} %all_gather.11), kind=kOutput, calls=%fused_computation.6 | convolution fusion | flops 805322752 | bytes 4751360 | tf_op jit(solution)/shard_map/dot_general | solution.py:55
  252.1 44.6 %psum.15 = bf16[256,64]{0,1:T(8,128)(2,1)S(1)} all-reduce(bf16[256,64]{0,1:T(8,128)(2,1)S(1)} %convolution_convert_fusion.3), channel_id=1, replica_groups=mesh['dp'=16,'pp'=16,'tp'=2] {'dp'}, use_global_device_ids=true, to_apply=%region_5.6 | all-reduce | flops 16384 | bytes 65536 | tf_op jit(solution)/shard_map/psum | solution.py:62
  296.7 0.6 multiply_bitcast_fusion
  297.3 0.0 collective-permute-done
  297.3 1.0 copy.11
  (6 shorter events, 0.0 us)
Async XLA Ops:
  7.2 47.9 %copy-start = (bf16[1,256,256]{2,1,0:T(8,128)(2,1)S(1)}, bf16[1,256,256]{2,1,0:T(8,128)(2,1)}, u32[]{:S(2)}) copy-start(bf16[1,256,256]{2,1,0:T(8,128)(2,1)} %param.6) | copy-start | bytes 393220
  7.2 47.9 %all-gather.7.cloned.1.call-start = ((), (), s32[]{:S(2)}) async-start(), calls=%async_computation.5 | async-start | bytes 3145728 | tf_op jit(solution)/shard_map/all_gather | solution.py:37
  7.9 94.6 %all-gather.5.cloned.1.call-start = ((), (), s32[]{:S(2)}) async-start(), calls=%async_computation.4 | async-start | bytes 2228224 | tf_op jit(solution)/shard_map/all_gather | solution.py:29
  8.7 51.4 %copy-start.2 = (f32[1,256,64]{1,2,0:T(8,128)S(1)}, f32[1,256,64]{1,2,0:T(8,128)}, u32[]{:S(2)}) copy-start(f32[1,256,64]{1,2,0:T(8,128)} %param.9) | copy-start | bytes 196612
  8.7 152.0 %reduce-scatter.5.cloned.1.call-start = ((), (), s32[]{:S(2)}) async-start(), calls=%async_computation.3 | async-start | bytes 557056 | tf_op jit(solution)/shard_map/reduce_scatter | solution.py:46
  58.1 1.9 copy-start.1
  65.0 154.6 %reduce-scatter.3.cloned.1.call-start = ((), (), s32[]{:S(2)}) async-start(), calls=%async_computation.2 | async-start | bytes 3145728 | tf_op jit(solution)/shard_map/reduce_scatter | solution.py:32
  219.6 77.7 %collective-permute-start = (bf16[256,2048]{1,0:T(8,128)(2,1)}, bf16[256,2048]{1,0:T(8,128)(2,1)S(1)}, u32[]{:S(2)}, u32[]{:S(2)}) collective-permute-start(bf16[256,2048]{1,0:T(8,128)(2,1)} %reduce-scatter.3.cloned.1.call-done), channel_id=1, source_target_pairs={{2,0},{4,2},{6,4},{8,6},{10,8},{12,10},{14,12},{16,14},{18,16},{20... | collective-permute-start | bytes 3145736 | tf_op jit(solution)/shard_map/ppermute | solution.py:12
Sparse Core Ops, SparseCore 0:
  10.1 44.9 all-gather.6
  57.2 45.2 all-gather.4
  105.9 54.7 reduce-scatter.4
  163.5 39.7 reduce-scatter.2
where the time goes:
time: 308 us; the launch traced here: 305 us
  waiting for transfers between devices  140 us (45%)
  blocking collectives  112 us (36%)
  matrix products  17.8 us (6%)
  between operations  13.9 us (5%)
  other arithmetic  12.7 us (4%)
  starting transfers between devices  5.5 us (2%)
    reduce_scatter x1, waiting for transfers between devices, on_device(): lax.psum_scatter(factor.astype(jnp.bfloat16), 'dp', scatter_dimension=0,...  54.5 us
    all_gather x1, waiting for transfers between devices, on_device(): inputs_whole = lax.all_gather(inputs_local, 'tp', axis=1, tiled=True)  46.4 us
    psum x1, blocking collectives, on_device(): lax.psum(jnp.dot(factor_rows.T, factor_rows, precision=HIGHEST), 'dp')  45.7 us
    psum x1, blocking collectives, on_device(): lax.psum(coeffs_local.astype(jnp.bfloat16), 'dp').astype(jnp.float32)  44.6 us
    all_gather x1, waiting for transfers between devices, on_device(): lax.all_gather(weight_local, 'dp', axis=0, tiled=True)  37.4 us
    all_gather x1, blocking collectives, on_device(): lax.all_gather(orthonormal(factor_rows, gram_matrix).astype(jnp.bfloat16)...  22 us
    another operation x3, other arithmetic, orthonormal(): lower_factor = jnp.linalg.cholesky(gram_matrix)  6.52 us
  transfers between devices with their start and end apart: 5, of which 3 were waited for; matrix products, arithmetic and copies ran while one was open for 10% of the time, Pallas kernels for 0%

commit v1 on v0

v1 whole, which is shorter than its diff:
```python
import jax
import jax.numpy as jnp
from jax import lax
from jax.experimental import pallas as pl
from jax.experimental.pallas import tpu as pltpu
from jax.sharding import Mesh
from jax.sharding import PartitionSpec as P

HIGHEST = lax.Precision.HIGHEST
BF16 = jnp.bfloat16
F32 = jnp.float32
GROUP = ("z", "c")


def swap(block, axis):
    return lax.ppermute(block, axis, [(0, 1), (1, 0)])


def dot(a, b, contract):
    return lax.dot_general(a, b, (contract, ((), ())), preferred_element_type=F32)


def split(values):
    high = values.astype(BF16)
    return jnp.concatenate([high, (values - high.astype(F32)).astype(BF16)], axis=1)


def finish_kernel(groups, gathered_ref, out_ref):
    rank = out_ref.shape[1]
    tall = out_ref.shape[0] // 2
    total = gathered_ref[0, :tall].astype(F32)
    for member in range(1, groups):
        total += gathered_ref[member, :tall].astype(F32)
    pair = gathered_ref[0, tall:].astype(F32) + gathered_ref[1, tall:].astype(F32)
    gram = pair[:, :rank] + pair[:, rank:]
    rows = lax.broadcasted_iota(jnp.int32, (rank, 2 * rank), 0)
    lanes = lax.broadcasted_iota(jnp.int32, (rank, 2 * rank), 1)
    identity = (lanes - rank == rows).astype(F32)
    work = jnp.concatenate([gram, gram], axis=1)
    work = jnp.where(lanes < rank, work, identity)
    for step in range(rank - 1):
        top = step // 8 * 8
        active = work[top:]
        column = jnp.broadcast_to(active[:, step : step + 1], active.shape)
        pivot_row = active[step - top : step - top + 1]
        pivot = column[step - top : step - top + 1]
        scaled = pivot_row / pivot
        active = active - jnp.where(rows[top:] > step, column, 0.0) * scaled
        work = active if top == 0 else jnp.concatenate([work[:top], active], axis=0)
    diagonal = jnp.sum(jnp.where(lanes == rows, work, 0.0), axis=1, keepdims=True)
    inverse = (work * lax.rsqrt(diagonal))[:, rank:]
    scale = 1.0 / groups
    for part in range(2):
        coeffs = total[:, part * rank : (part + 1) * rank] * scale
        out_ref[part * tall : (part + 1) * tall] = lax.dot_general(
            coeffs, inverse, (((1,), (1,)), ((), ())), precision=HIGHEST, preferred_element_type=F32
        )


def finish(gathered, kept, rank):
    return pl.pallas_call(
        lambda gathered_ref, out_ref: finish_kernel(gathered.shape[0], gathered_ref, out_ref),
        out_shape=jax.ShapeDtypeStruct((kept, rank), F32),
        name="finish",
    )(gathered)


def weight_route(chips, cores, sections):
    half = chips // 2

    def index(z, c, s, t):
        return ((z * cores + c) * sections + s) * 2 + t

    route = []
    for s in range(sections - 1):
        for z in range(chips):
            for c in range(cores):
                for t in range(2):
                    source = index(half * t + z % half, c, s + 1, t if z < half else 1 - t)
                    route.append((source, index(z, c, s, t)))
    return route


def on_device(activations, key_grads, key_weight, error_buf, q_prev):
    chips, cores, sections = (lax.axis_size(name) for name in ("z", "c", "pp"))
    groups = chips * cores
    core, side = lax.axis_index("c"), lax.axis_index("tp")
    inputs_local, grads_local, weight_local = activations[0], key_grads[0], key_weight[0]
    rank = q_prev.shape[2]
    tokens, features = inputs_local.shape
    part = features // cores
    columns = grads_local.shape[1]
    error_local = error_buf[0, 0].reshape(2, cores, part, columns)

    packed = jnp.concatenate([grads_local, split(q_prev[0])], axis=1)
    packed_near = swap(packed, "tp")
    inputs_mine = lax.dynamic_slice_in_dim(inputs_local, core * part, part, 1)
    inputs_other = lax.dynamic_slice_in_dim(inputs_local, (1 - core) * part, part, 1)
    inputs_pair = swap(inputs_other, "c")
    error_mine = lax.dynamic_index_in_dim(error_local, core, 1, keepdims=False)
    error_other = lax.dynamic_index_in_dim(error_local, 1 - core, 1, keepdims=False)
    error_pair = swap(error_other, "c")
    q_own, q_near = packed[:, columns:], packed_near[:, columns:]
    grads_near = packed_near[:, :columns]
    grads_both = jnp.stack([grads_local, grads_near])
    grads_pair = swap(grads_both, "c")

    weight_piece = lax.ppermute(
        weight_local, ("z", "c", "pp", "tp"), weight_route(chips, cores, sections)
    )
    weight_all = lax.all_gather(weight_piece, GROUP, axis=0, tiled=False)
    grads_next = lax.ppermute(grads_both, "pp", [(i, i - 1) for i in range(1, sections)])
    weight_own = weight_all[: groups // 2].reshape(features, columns)
    weight_near = weight_all[groups // 2 :].reshape(features, columns)
    grad_prev = (
        dot(grads_next[0], weight_own, ((1,), (1,))) + dot(grads_next[1], weight_near, ((1,), (1,)))
    ).astype(BF16)

    tall = ((0,), (0,))
    product_near = (
        dot(inputs_mine, grads_near, tall) + dot(inputs_pair, grads_pair[1], tall)
    ).astype(BF16)
    product_own = (
        dot(inputs_mine, grads_local, tall) + dot(inputs_pair, grads_pair[0], tall)
    ).astype(BF16)
    wide = ((1,), (0,))

    def times_q(block, q):
        both = dot(block, q, wide)
        return both[:, :rank] + both[:, rank:]

    factor_from_near = swap(times_q(product_near, q_near).astype(BF16), "tp").astype(F32)
    product_from_near = swap(product_near, "tp")
    factor_own = times_q(product_own, q_own)
    factor_error = [
        times_q(error_mine[half], q_own) + times_q(error_pair[half], q_own) for half in range(2)
    ]
    first = side == 0
    factor = jnp.concatenate(
        [
            factor_error[0] + jnp.where(first, factor_own, factor_from_near),
            factor_error[1] + jnp.where(first, factor_from_near, factor_own),
        ],
        axis=1,
    )
    shares = (factor / groups).astype(BF16).reshape(chips, part // chips, 2 * rank)
    shares = lax.all_to_all(shares, "z", 0, 0)
    share = jnp.sum(shares.astype(F32), axis=0).astype(BF16)
    factor = lax.all_to_all(jnp.broadcast_to(share, (chips, *share.shape)), "z", 0, 0)
    factor = factor.reshape(part, 2 * rank)

    gram_pair = dot(factor, factor, tall)
    gram = gram_pair[:rank, :rank] + gram_pair[rank:, rank:]
    product = [
        jnp.where(first, product_own, product_from_near),
        jnp.where(first, product_from_near, product_own),
    ]
    coeffs = 0.0
    for half in range(2):
        summed = (
            error_mine[half].astype(F32) + error_pair[half].astype(F32) + product[half].astype(F32)
        ).astype(BF16)
        coeffs += dot(summed, factor[:, half * rank : (half + 1) * rank], tall)
    kept = columns // 2
    coeffs = jnp.concatenate([coeffs[:kept], coeffs[kept:]], axis=1).astype(BF16)
    payload = jnp.concatenate([coeffs, split(gram)], axis=0)
    gathered = lax.all_gather(payload, GROUP, axis=0, tiled=False)
    return (grad_prev[None], finish(gathered, columns, rank)[None])


def solution(mesh):
    groups, sections, sides = (mesh.shape[name] for name in ("dp", "pp", "tp"))
    split_mesh = Mesh(
        mesh.devices.reshape(groups // 2, 2, sections, sides), ("z", "c", "pp", "tp")
    )
    return jax.shard_map(
        on_device,
        mesh=split_mesh,
        in_specs=(
            P("pp", GROUP, "tp"),
            P("pp", GROUP, "tp"),
            P("pp", GROUP, "tp"),
            P("pp", GROUP, None, "tp"),
            P("pp", "tp", None),
        ),
        out_specs=(P("pp", GROUP, "tp"), P("pp", "tp", None)),
        check_vma=False,
    )
```

time: 308 us -> 140 us (0.45)
  the two profiles are of different devices: /device:TPU:7 before, /device:TPU:61 now
where the time goes in v1:
time: 140 us
  blocking collectives  41.1 us (29%)
  starting transfers between devices  33 us (24%)
  matrix products  17.7 us (13%)
  waiting for transfers between devices  15 us (11%)
  between operations  14.4 us (10%)
  local copies, waits for them, and re-layouts  7.54 us (5%)
  Pallas kernels  7.53 us (5%)
  other arithmetic  3.32 us (2%)
    ppermute x6, starting transfers between devices, swap(): return lax.ppermute(block, axis, [(0, 1), (1, 0)])  23.7 us
    all_gather x1, blocking collectives, on_device(): gathered = lax.all_gather(payload, GROUP, axis=0, tiled=False)  22.2 us
    all_to_all x1, blocking collectives, on_device(): shares = lax.all_to_all(shares, 'z', 0, 0)  18.9 us
    dot_general x15, matrix products, dot(): lax.dot_general(a, b, (contract, ((), ())), preferred_element_type=F32)  17.7 us
    all_to_all x1, waiting for transfers between devices, on_device(): lax.all_to_all(jnp.broadcast_to(share, (chips, *share.shape)), 'z', 0, 0)  7.92 us
    pallas_call x1, Pallas kernels, finish(): pl.pallas_call(lambda gathered_ref, out_ref: finish_kernel(gathered.shape...  7.53 us
    ppermute x6, waiting for transfers between devices, swap(): return lax.ppermute(block, axis, [(0, 1), (1, 0)])  7.03 us
    all_to_all x1, starting transfers between devices, on_device(): lax.all_to_all(jnp.broadcast_to(share, (chips, *share.shape)), 'z', 0, 0)  3.41 us
  transfers between devices with their start and end apart: 10, of which 2 were waited for; matrix products, arithmetic and copies ran while one was open for 15% of the time, Pallas kernels for 5%

profile of v1, /device:TPU:61, one launch (start us, length us, event | category | flops | bytes accessed | tf_op | source)
XLA Modules:
  0.0 139.6 jit_solution(15867815846365957769)
XLA Ops:
  7.2 0.9 bitcast_convert_fusion
  8.2 0.9 fusion.36
  9.3 1.0 pad_maximum_fusion.1
  10.3 2.8 %collective-permute-start = (bf16[256,384]{1,0:T(8,128)(2,1)S(1)}, bf16[256,384]{1,0:T(8,128)(2,1)S(1)}, u32[]{:S(2)}, u32[]{:S(2)}) collective-permute-start(bf16[256,384]{1,0:T(8,128)(2,1)S(1)} %pad_maximum_fusion.1), channel_id=1, source_target_pairs={{0,1},{1,0},{2,3},{3,2},{4,5},{5,4},{6,7},{7,6},{8,9},{9,8},{10,11... | collective-permute-start | bytes 589832 | tf_op jit(solution)/shard_map/ppermute | solution.py:16
  13.1 0.9 dynamic-slice_bitcast_fusion.3
  14.0 2.9 %collective-permute-start.4 = (bf16[256,1024]{1,0:T(8,128)(2,1)}, bf16[256,1024]{1,0:T(8,128)(2,1)S(1)}, u32[]{:S(2)}, u32[]{:S(2)}) collective-permute-start(bf16[256,1024]{1,0:T(8,128)(2,1)} %dynamic-slice_bitcast_fusion.3), channel_id=1, source_target_pairs={{0,32},{32,0},{1,33},{33,1},{2,34},{34,2},{3,35},{35,3},{4,36},{36... | collective-permute-start | bytes 1572872 | tf_op jit(solution)/shard_map/ppermute | solution.py:16
  16.8 2.3 %dynamic-slice_bitcast_fusion = bf16[2,1024,256]{2,1,0:T(8,128)(2,1)} fusion(bf16[2,2,1024,256]{3,2,1,0:T(8,128)(2,1)} %bitcast.85, s32[]{:T(128)S(6)} %select_n.38), kind=kLoop, calls=%fused_computation.15 | loop fusion | bytes 2097156 | tf_op jit(solution)/shard_map/jit(dynamic_index_in_dim)/squeeze | solution.py:101
  19.1 1.9 %collective-permute-start.3 = (bf16[2,1024,256]{2,1,0:T(8,128)(2,1)}, bf16[2,1024,256]{2,1,0:T(8,128)(2,1)}, u32[]{:S(2)}, u32[]{:S(2)}) collective-permute-start(bf16[2,1024,256]{2,1,0:T(8,128)(2,1)} %dynamic-slice_bitcast_fusion), channel_id=1, source_target_pairs={{0,32},{32,0},{1,33},{33,1},{2,34},{34,2},{3,35},{35,3},{4,36},{36... | collective-permute-start | bytes 3145736 | tf_op jit(solution)/shard_map/ppermute | solution.py:16
  21.0 3.0 %collective-permute-start.2 = (bf16[256,256]{1,0:T(8,128)(2,1)}, bf16[256,256]{1,0:T(8,128)(2,1)S(1)}, u32[]{:S(2)}, u32[]{:S(2)}) collective-permute-start(bf16[256,256]{1,0:T(8,128)(2,1)} %bitcast.4), channel_id=1, source_target_pairs={{2,0},{259,1},{34,32},{291,33},{66,64},{323,65},{98,96},{355,97},{... | collective-permute-start | bytes 393224 | tf_op jit(solution)/shard_map/ppermute | solution.py:108
  24.1 2.7 %collective-permute-start.5 = (bf16[2,256,256]{2,1,0:T(8,128)(2,1)S(1)}, bf16[2,256,256]{2,1,0:T(8,128)(2,1)}, u32[]{:S(2)}, u32[]{:S(2)}) collective-permute-start(bf16[2,256,256]{2,1,0:T(8,128)(2,1)S(1)} %pad_maximum_fusion), channel_id=1, source_target_pairs={{0,32},{32,0},{1,33},{33,1},{2,34},{34,2},{3,35},{35,3},{4,36},{36... | collective-permute-start | bytes 786440 | tf_op jit(solution)/shard_map/ppermute | solution.py:16
  27.2 2.1 %fusion.19 = f32[1024,128]{0,1:T(8,128)} fusion(bf16[2,2,1024,256]{3,2,1,0:T(8,128)(2,1)} %bitcast.86, s32[]{:T(128)S(6)} %select_n.37, bf16[256,64]{0,1:T(8,128)(2,1)S(1)} %fusion.36, bf16[256,64]{0,1:T(8,128)(2,1)S(1)} %bitcast_convert_fusion), kind=kOutput, calls=%fused_computation.33 | convolution fusion | flops 67239936 | bytes 1114116 | tf_op jit(solution)/shard_map/dot_general | solution.py:20
  29.3 2.1 %fusion.22 = f32[1024,128]{0,1:T(8,128)} fusion(bf16[2,2,1024,256]{3,2,1,0:T(8,128)(2,1)} %bitcast.87, s32[]{:T(128)S(6)} %add.94, s32[]{:T(128)S(6)} %select_n.37, bf16[256,64]{0,1:T(8,128)(2,1)S(1)} %fusion.36, bf16[256,64]{0,1:T(8,128)(2,1)S(1)} %bitcast_convert_fusion), kind=kOutput, calls=%fused_computation.36 | convolution fusion | flops 67239936 | bytes 1114120 | tf_op jit(solution)/shard_map/dot_general | solution.py:20
  32.2 1.3 fusion.32
  34.1 11.5 %collective-permute-start.7 = (bf16[1024,64]{0,1:T(8,128)(2,1)S(1)}, bf16[1024,64]{0,1:T(8,128)(2,1)S(1)}, u32[]{:S(2)}, u32[]{:S(2)}) collective-permute-start(bf16[1024,64]{0,1:T(8,128)(2,1)S(1)} %fusion.30), channel_id=1, source_target_pairs={{0,1},{1,0},{2,3},{3,2},{4,5},{5,4},{6,7},{7,6},{8,9},{9,8},{10,11... | collective-permute-start | bytes 393224 | tf_op jit(solution)/shard_map/ppermute | solution.py:16
  45.7 1.3 fusion.2
  47.0 0.8 copy-done.1
  48.1 1.3 fusion.17
  49.4 1.3 fusion.18
  51.2 18.9 %all_to_all.10 = bf16[8,128,128]{1,2,0:T(8,128)(2,1)S(1)} all-to-all(bf16[8,128,128]{1,2,0:T(8,128)(2,1)S(1)} %fusion.9), channel_id=1, replica_groups=mesh['z'=8,'c'=2,'pp'=16,'tp'=2] {'z'}, dimensions={0} | all-to-all | bytes 524288 | tf_op jit(solution)/shard_map/all_to_all | solution.py:147
  70.2 0.7 broadcast_in_dim.10
  71.0 3.4 %all-to-all-start.1 = ((bf16[8,128,128]{2,1,0:T(8,128)(2,1)}), bf16[8,128,128]{2,1,0:T(8,128)(2,1)S(1)}, u32[]{:S(2)}, u32[]{:S(2)}) async-start(bf16[8,128,128]{2,1,0:T(8,128)(2,1)} %broadcast_in_dim.10), calls=%async_computation.1 | async-start | bytes 524288 | tf_op jit(solution)/shard_map/all_to_all | solution.py:149
  74.4 1.9 %collective-permute-start.6 = (bf16[1024,256]{1,0:T(8,128)(2,1)S(1)}, bf16[1024,256]{1,0:T(8,128)(2,1)S(1)}, u32[]{:S(2)}, u32[]{:S(2)}) collective-permute-start(bf16[1024,256]{1,0:T(8,128)(2,1)S(1)} %fusion.3), channel_id=1, source_target_pairs={{0,1},{1,0},{2,3},{3,2},{4,5},{5,4},{6,7},{7,6},{8,9},{9,8},{10,11... | collective-permute-start | bytes 1572872 | tf_op jit(solution)/shard_map/ppermute | solution.py:16
  76.4 2.9 %collective-permute-start.1 = (bf16[2,256,256]{2,1,0:T(8,128)(2,1)S(1)}, bf16[2,256,256]{2,1,0:T(8,128)(2,1)S(1)}, u32[]{:S(2)}, u32[]{:S(2)}) collective-permute-start(bf16[2,256,256]{2,1,0:T(8,128)(2,1)S(1)} %copy-done.8), channel_id=1, source_target_pairs={{2,0},{4,2},{6,4},{8,6},{10,8},{12,10},{14,12},{16,14},{18,16},{20... | collective-permute-start | bytes 786440 | tf_op jit(solution)/shard_map/ppermute | solution.py:112
  79.2 7.9 %all-to-all-done.1 = bf16[8,128,128]{2,1,0:T(8,128)(2,1)S(1)} async-done(((bf16[8,128,128]{2,1,0:T(8,128)(2,1)}), bf16[8,128,128]{2,1,0:T(8,128)(2,1)S(1)}, u32[]{:S(2)}, u32[]{:S(2)}) %all-to-all-start.1) | async-done | bytes 262176 | tf_op jit(solution)/shard_map/all_to_all | solution.py:149
  87.4 7.0 %collective-permute-done.6 = bf16[1024,256]{1,0:T(8,128)(2,1)S(1)} collective-permute-done((bf16[1024,256]{1,0:T(8,128)(2,1)S(1)}, bf16[1024,256]{1,0:T(8,128)(2,1)S(1)}, u32[]{:S(2)}, u32[]{:S(2)}) %collective-permute-start.6) | collective-permute-done | bytes 524320 | tf_op jit(solution)/shard_map/ppermute | solution.py:16
  94.4 1.7 %fusion.8 = f32[256,64]{0,1:T(8,128)S(1)} fusion(bf16[1024,256]{1,0:T(8,128)(2,1)S(1)} %collective-permute-done.6, bf16[1024,256]{1,0:T(8,128)(2,1)S(1)} %copy-done.2, pred[]{:T(512)S(6)} %eq.3, bf16[2,1024,256]{2,1,0:T(8,128)(2,1)} %collective-permute-done.3, bf16[2,2,1024,256]{3,2,1,0:T(8,128)(2,1)} %bitcast.88, s32[]{:T(128)S(6)} %add.94, ...), kind=kOutput, calls=%fused_computation.16 | convolution fusion | flops 35389440 | bytes 2424841 | tf_op jit(solution)/shard_map/dot_general | solution.py:20
  96.1 1.6 %fusion.4 = bf16[256,64]{0,1:T(8,128)(2,1)S(1)} fusion(f32[256,64]{0,1:T(8,128)S(1)} %fusion.8, bf16[1024,256]{1,0:T(8,128)(2,1)S(1)} %copy-done.2, bf16[1024,256]{1,0:T(8,128)(2,1)S(1)} %collective-permute-done.6, pred[]{:T(512)S(6)} %eq.3, bf16[2,1024,256]{2,1,0:T(8,128)(2,1)} %collective-permute-done.3, bf16[2,2,1024,256]{3,2,1,0:T(8,128)(2,1)} %bitcast.89, ...), kind=kOutput, calls=%fused_computation.9 | convolution fusion | flops 35422208 | bytes 2457605 | tf_op jit(solution)/shard_map/dot_general | solution.py:20
  98.0 22.2 %all-gather.1 = bf16[3072,128]{1,0:T(8,128)(2,1)} all-gather(bf16[192,128]{1,0:T(8,128)(2,1)S(1)} %copy.23), channel_id=3, replica_groups=mesh['z'=8,'c'=2,'pp'=16,'tp'=2] {'z','c'}, dimensions={0}, use_global_device_ids=true | all-gather | bytes 835584 | tf_op jit(solution)/shard_map/all_gather | solution.py:167
  120.2 7.5 %finish.1 = f32[256,64]{1,0:T(8,128)} custom-call(bf16[16,192,128]{2,1,0:T(8,128)(2,1)} %bitcast.82), custom_call_target="tpu_custom_call" | custom-call | tf_op jit(solution)/shard_map/finish/pallas_call | solution.py:61
  127.8 1.6 %copy.24 = f32[1,256,64]{1,2,0:T(8,128)} copy(f32[1,256,64]{2,1,0:T(8,128)} %bitcast.91) | data formatting | bytes 131072
  129.4 1.8 %fusion.5 = f32[256,2048]{1,0:T(8,128)S(1)} fusion(bf16[4096,256]{1,0:T(8,128)(2,1)} %all-gather.4.cloned.1.call-done, bf16[2,256,256]{2,1,0:T(8,128)(2,1)S(1)} %collective-permute-done.1), kind=kOutput, calls=%fused_computation.10 | convolution fusion | flops 268435456 | bytes 3276800 | tf_op jit(solution)/shard_map/dot_general | solution.py:20
  131.3 1.5 %fusion.1 = bf16[1,256,2048]{2,1,0:T(8,128)(2,1)} fusion(f32[256,2048]{1,0:T(8,128)S(1)} %fusion.5, bf16[4096,256]{1,0:T(8,128)(2,1)S(1)} %copy-done.3, bf16[2,256,256]{2,1,0:T(8,128)(2,1)S(1)} %collective-permute-done.1), kind=kOutput, calls=%fused_computation.2 | convolution fusion | flops 269484032 | bytes 4325376 | tf_op jit(solution)/shard_map/dot_general | solution.py:20
  (48 shorter events, 3.4 us)
Async XLA Ops:
  7.2 6.0 %copy-start = (bf16[1,256,2048]{2,1,0:T(8,128)(2,1)S(1)}, bf16[1,256,2048]{2,1,0:T(8,128)(2,1)}, u32[]{:S(2)}) copy-start(bf16[1,256,2048]{2,1,0:T(8,128)(2,1)} %param.5) | copy-start | bytes 3145732
  7.2 122.2 %all-gather.4.cloned.1.call-start = ((), (), s32[]{:S(2)}) async-start(), calls=%async_computation.2 | async-start | bytes 2228224 | tf_op jit(solution)/shard_map/all_gather | solution.py:111
  8.1 15.9 %copy-start.6 = (bf16[1,256,256]{2,1,0:T(8,128)(2,1)S(1)}, bf16[1,256,256]{2,1,0:T(8,128)(2,1)}, u32[]{:S(2)}) copy-start(bf16[1,256,256]{2,1,0:T(8,128)(2,1)} %param.6) | copy-start | bytes 393220
  10.3 13.7 %collective-permute-start = (bf16[256,384]{1,0:T(8,128)(2,1)S(1)}, bf16[256,384]{1,0:T(8,128)(2,1)S(1)}, u32[]{:S(2)}, u32[]{:S(2)}) collective-permute-start(bf16[256,384]{1,0:T(8,128)(2,1)S(1)} %pad_maximum_fusion.1), channel_id=1, source_target_pairs={{0,1},{1,0},{2,3},{3,2},{4,5},{5,4},{6,7},{7,6},{8,9},{9,8},{10,11... | collective-permute-start | bytes 589832 | tf_op jit(solution)/shard_map/ppermute | solution.py:16
  14.0 18.2 %collective-permute-start.4 = (bf16[256,1024]{1,0:T(8,128)(2,1)}, bf16[256,1024]{1,0:T(8,128)(2,1)S(1)}, u32[]{:S(2)}, u32[]{:S(2)}) collective-permute-start(bf16[256,1024]{1,0:T(8,128)(2,1)} %dynamic-slice_bitcast_fusion.3), channel_id=1, source_target_pairs={{0,32},{32,0},{1,33},{33,1},{2,34},{34,2},{3,35},{35,3},{4,36},{36... | collective-permute-start | bytes 1572872 | tf_op jit(solution)/shard_map/ppermute | solution.py:16
  19.1 28.9 %collective-permute-start.3 = (bf16[2,1024,256]{2,1,0:T(8,128)(2,1)}, bf16[2,1024,256]{2,1,0:T(8,128)(2,1)}, u32[]{:S(2)}, u32[]{:S(2)}) collective-permute-start(bf16[2,1024,256]{2,1,0:T(8,128)(2,1)} %dynamic-slice_bitcast_fusion), channel_id=1, source_target_pairs={{0,32},{32,0},{1,33},{33,1},{2,34},{34,2},{3,35},{35,3},{4,36},{36... | collective-permute-start | bytes 3145736 | tf_op jit(solution)/shard_map/ppermute | solution.py:16
  21.0 10.4 %collective-permute-start.2 = (bf16[256,256]{1,0:T(8,128)(2,1)}, bf16[256,256]{1,0:T(8,128)(2,1)S(1)}, u32[]{:S(2)}, u32[]{:S(2)}) collective-permute-start(bf16[256,256]{1,0:T(8,128)(2,1)} %bitcast.4), channel_id=1, source_target_pairs={{2,0},{259,1},{34,32},{291,33},{66,64},{323,65},{98,96},{355,97},{... | collective-permute-start | bytes 393224 | tf_op jit(solution)/shard_map/ppermute | solution.py:108
  24.1 8.1 %copy-start.7 = (bf16[2,256,256]{2,1,0:T(8,128)(2,1)}, bf16[2,256,256]{2,1,0:T(8,128)(2,1)S(1)}, u32[]{:S(2)}) copy-start(bf16[2,256,256]{2,1,0:T(8,128)(2,1)S(1)} %pad_maximum_fusion) | copy-start | bytes 786436
  24.1 8.0 %collective-permute-start.5 = (bf16[2,256,256]{2,1,0:T(8,128)(2,1)S(1)}, bf16[2,256,256]{2,1,0:T(8,128)(2,1)}, u32[]{:S(2)}, u32[]{:S(2)}) collective-permute-start(bf16[2,256,256]{2,1,0:T(8,128)(2,1)S(1)} %pad_maximum_fusion), channel_id=1, source_target_pairs={{0,32},{32,0},{1,33},{33,1},{2,34},{34,2},{3,35},{35,3},{4,36},{36... | collective-permute-start | bytes 786440 | tf_op jit(solution)/shard_map/ppermute | solution.py:16
  31.5 0.7 copy-start.9
  34.1 16.6 %collective-permute-start.7 = (bf16[1024,64]{0,1:T(8,128)(2,1)S(1)}, bf16[1024,64]{0,1:T(8,128)(2,1)S(1)}, u32[]{:S(2)}, u32[]{:S(2)}) collective-permute-start(bf16[1024,64]{0,1:T(8,128)(2,1)S(1)} %fusion.30), channel_id=1, source_target_pairs={{0,1},{1,0},{2,3},{3,2},{4,5},{5,4},{6,7},{7,6},{8,9},{9,8},{10,11... | collective-permute-start | bytes 393224 | tf_op jit(solution)/shard_map/ppermute | solution.py:16
  46.9 0.8 copy-start.1
  47.7 3.0 %copy-start.4 = (f32[1024,128]{0,1:T(8,128)S(1)}, f32[1024,128]{0,1:T(8,128)}, u32[]{:S(2)}) copy-start(f32[1024,128]{0,1:T(8,128)} %fusion.22) | copy-start | bytes 1572868
  47.7 3.0 %copy-start.5 = (f32[1024,128]{0,1:T(8,128)S(1)}, f32[1024,128]{0,1:T(8,128)}, u32[]{:S(2)}) copy-start(f32[1024,128]{0,1:T(8,128)} %fusion.19) | copy-start | bytes 1572868
  51.1 25.3 %copy-start.8 = (bf16[2,256,256]{2,1,0:T(8,128)(2,1)S(1)}, bf16[2,256,256]{2,1,0:T(8,128)(2,1)}, u32[]{:S(2)}) copy-start(bf16[2,256,256]{2,1,0:T(8,128)(2,1)} %copy-done.7) | copy-start | bytes 786436
  51.1 43.4 %copy-start.2 = (bf16[1024,256]{1,0:T(8,128)(2,1)S(1)}, bf16[1024,256]{1,0:T(8,128)(2,1)}, u32[]{:S(2)}) copy-start(bf16[1024,256]{1,0:T(8,128)(2,1)} %copy-done.1) | copy-start | bytes 1572868
  71.0 16.2 %all-to-all-start.1 = ((bf16[8,128,128]{2,1,0:T(8,128)(2,1)}), bf16[8,128,128]{2,1,0:T(8,128)(2,1)S(1)}, u32[]{:S(2)}, u32[]{:S(2)}) async-start(bf16[8,128,128]{2,1,0:T(8,128)(2,1)} %broadcast_in_dim.10), calls=%async_computation.1 | async-start | bytes 524288 | tf_op jit(solution)/shard_map/all_to_all | solution.py:149
  74.4 20.0 %collective-permute-start.6 = (bf16[1024,256]{1,0:T(8,128)(2,1)S(1)}, bf16[1024,256]{1,0:T(8,128)(2,1)S(1)}, u32[]{:S(2)}, u32[]{:S(2)}) collective-permute-start(bf16[1024,256]{1,0:T(8,128)(2,1)S(1)} %fusion.3), channel_id=1, source_target_pairs={{0,1},{1,0},{2,3},{3,2},{4,5},{5,4},{6,7},{7,6},{8,9},{9,8},{10,11... | collective-permute-start | bytes 1572872 | tf_op jit(solution)/shard_map/ppermute | solution.py:16
  76.4 53.0 %collective-permute-start.1 = (bf16[2,256,256]{2,1,0:T(8,128)(2,1)S(1)}, bf16[2,256,256]{2,1,0:T(8,128)(2,1)S(1)}, u32[]{:S(2)}, u32[]{:S(2)}) collective-permute-start(bf16[2,256,256]{2,1,0:T(8,128)(2,1)S(1)} %copy-done.8), channel_id=1, source_target_pairs={{2,0},{4,2},{6,4},{8,6},{10,8},{12,10},{14,12},{16,14},{18,16},{20... | collective-permute-start | bytes 786440 | tf_op jit(solution)/shard_map/ppermute | solution.py:112
  129.4 1.9 %copy-start.3 = (bf16[4096,256]{1,0:T(8,128)(2,1)S(1)}, bf16[4096,256]{1,0:T(8,128)(2,1)}, u32[]{:S(2)}) copy-start(bf16[4096,256]{1,0:T(8,128)(2,1)} %all-gather.4.cloned.1.call-done) | copy-start | bytes 6291460
Sparse Core Ops, SparseCore 0:
  32.2 56.8 all-gather.3

commit v2 on v0

v2 whole, which is shorter than its diff:
```python
import jax
import jax.numpy as jnp
from jax import lax
from jax.experimental import pallas as pl
from jax.experimental.pallas import tpu as pltpu
from jax.sharding import Mesh
from jax.sharding import PartitionSpec as P

HIGHEST = lax.Precision.HIGHEST
BF16 = jnp.bfloat16
F32 = jnp.float32
GROUP = ("z", "c")
VMEM_LIMIT = 12 * 2**20
VMEM_ALL = 60 * 2**20
STEP = 512
WIDE = 4


def swap(block, axis):
    return lax.ppermute(block, axis, [(0, 1), (1, 0)])


def dot(a, b, a_dim=1, b_dim=0):
    return lax.dot_general(a, b, (((a_dim,), (b_dim,)), ((), ())), preferred_element_type=F32)


def split(values, axis):
    high = values.astype(BF16)
    return jnp.concatenate([high, (values - high.astype(F32)).astype(BF16)], axis=axis)


def place(name):
    return lax.axis_index(name).astype(jnp.int32).reshape(1)


def call(kernel, out_shapes, name, operands, scalars=1, flops=10**8, moved=4 * 10**6):
    spaces = [pltpu.SMEM] * scalars + [pltpu.VMEM] * (len(operands) - scalars)
    return pl.pallas_call(
        kernel,
        out_shape=out_shapes,
        in_specs=[pl.BlockSpec(memory_space=space) for space in spaces],
        cost_estimate=pl.CostEstimate(flops=flops, bytes_accessed=moved, transcendentals=0),
        compiler_params=pltpu.CompilerParams(vmem_limit_bytes=VMEM_LIMIT),
        name=name,
    )(*operands)


def times_q(q_parts, block):
    rank = q_parts.shape[0] // 2
    both = dot(q_parts, block, 1, 1)
    return both[:rank] + both[rank:]


def project_kernel(
    side_ref, q_hbm, grads_hbm, error_hbm, payload_ref, q_ref, grads_ref, error_ref, arrived
):
    features, tokens = error_ref.shape[0], grads_ref.shape[0]
    away = pl.ds(pl.multiple_of((1 - side_ref[0]) * features, features), features)
    sources = (q_hbm, grads_hbm, error_hbm.at[away])
    targets = (q_ref, grads_ref, error_ref)
    copies = [pltpu.make_async_copy(*sources_targets, arrived.at[i])
              for i, sources_targets in enumerate(zip(sources, targets))]
    for copy in copies:
        copy.start()
    copies[0].wait()
    q_parts = split(q_ref[...], 0)
    copies[1].wait()
    payload_ref[:, features:] = times_q(q_parts, grads_ref[...]).astype(BF16)
    copies[2].wait()
    for start in range(0, features, STEP):
        rows = slice(start, start + STEP)
        payload_ref[:, rows] = times_q(q_parts, error_ref[rows]).astype(BF16)


def project(side, q_prev, grads, error):
    rank, columns = q_prev.shape
    tokens, features = grads.shape[0], error.shape[0] // 2
    hbm = pl.BlockSpec(memory_space=pltpu.HBM)
    return pl.pallas_call(
        project_kernel,
        out_shape=jax.ShapeDtypeStruct((rank, features + tokens), BF16),
        in_specs=[pl.BlockSpec(memory_space=pltpu.SMEM), hbm, hbm, hbm],
        out_specs=pl.BlockSpec(memory_space=pltpu.VMEM),
        scratch_shapes=[
            pltpu.VMEM((rank, columns), F32),
            pltpu.VMEM((tokens, columns), BF16),
            pltpu.VMEM((features, columns), BF16),
            pltpu.SemaphoreType.DMA((3,)),
        ],
        cost_estimate=pl.CostEstimate(flops=10**8, bytes_accessed=2 * 10**6, transcendentals=0),
        compiler_params=pltpu.CompilerParams(vmem_limit_bytes=VMEM_ALL),
        name="project",
    )(side, q_prev, grads, error)


def left_kernel(groups, side_ref, pair_ref, q_ref, error_ref, inputs_ref, out_ref):
    features, side = inputs_ref.shape[1], side_ref[0]
    rank = q_ref.shape[0]
    payload_ref, near_ref = pair_ref.at[side], pair_ref.at[1 - side]
    q_parts = split(q_ref[...], 0)
    mixed = jnp.concatenate([payload_ref[:, features:], near_ref[:, features:]], axis=0)
    for start in range(0, features, STEP):
        lanes = slice(start, start + STEP)
        rows = pl.ds(pl.multiple_of(side * features + start, STEP), STEP)
        product = dot(mixed, inputs_ref[:, lanes])
        own = (product[:rank] + times_q(q_parts, error_ref[rows])) * (1.0 / groups)
        near = (product[rank:] + near_ref[:, lanes].astype(F32)) * (1.0 / groups)
        out_ref[0, :, lanes] = own.astype(BF16)
        out_ref[1, :, lanes] = near.astype(BF16)


def chip_sum_kernel(pair_ref, out_ref):
    chunks, _, width = out_ref.shape
    for chunk in range(chunks):
        lanes = slice(chunk * width, (chunk + 1) * width)
        total = pair_ref[0, :, lanes].astype(F32) + pair_ref[1, :, lanes].astype(F32)
        out_ref[chunk] = total.astype(BF16)


def share_kernel(shares_ref, out_ref):
    groups = shares_ref.shape[0]
    for core in range(2):
        total = shares_ref[core].astype(F32)
        for member in range(core + 2, groups, 2):
            total += shares_ref[member].astype(F32)
        total = total.astype(BF16)
        for member in range(core, groups, 2):
            out_ref[member] = total


def right_kernel(
    side_ref, factor_ref, inputs_ref, near_ref, error_ref, away_ref, projected_ref, own_ref, gram_ref
):
    _, chunks, rank, width = factor_ref.shape
    side = side_ref[0]
    tokens, features = inputs_ref.shape
    columns = own_ref.shape[1]
    projected = jnp.zeros((2 * rank, tokens), F32)
    gram = jnp.zeros((2 * rank, 2 * rank), F32)
    own = jnp.zeros((rank, columns), F32)
    near = jnp.zeros((rank, columns), F32)
    for chunk in range(0, chunks, 2):
        factor = jnp.concatenate(
            [
                jnp.concatenate([factor_ref[block, chunk + i] for i in range(2)], axis=1)
                for block in range(2)
            ],
            axis=0,
        )
        lanes = slice(chunk * width, (chunk + 2) * width)
        projected += dot(factor, inputs_ref[:, lanes], 1, 1)
        gram += dot(factor, factor, 1, 1)
        near += dot(factor[rank:], near_ref[lanes])
        start, size = chunk * width, 2 * width
        rows = pl.ds(pl.multiple_of(side * features + start, size), size)
        own += dot(factor[:rank], error_ref[rows])
    away_ref[:, :tokens] = projected[rank:].astype(BF16)
    away_ref[:, tokens : tokens + columns] = near.astype(BF16)
    away_ref[:, tokens + columns :] = split(gram[rank:, rank:], 1)
    projected_ref[...] = projected[:rank]
    own_ref[...] = own
    gram_ref[...] = gram[:rank, :rank]


def join_kernel(side_ref, pair_ref, projected_ref, own_ref, grads_ref, out_ref):
    tokens, columns = grads_ref.shape
    near = pair_ref[1 - side_ref[0]].astype(F32)
    projected = (projected_ref[...] + near[:, :tokens]).astype(BF16)
    total = own_ref[...] + near[:, tokens : tokens + columns]
    out_ref[...] = (total + dot(projected, grads_ref[...])).astype(BF16)


def spread_kernel(core_ref, pair_ref, out_ref):
    copies, _, width = out_ref.shape
    lanes = pl.ds(pl.multiple_of(core_ref[0] * width, width), width)
    total = pair_ref[0, :, lanes].astype(F32) + pair_ref[1, :, lanes].astype(F32)
    total = total.astype(BF16)
    for copy in range(copies):
        out_ref[copy] = total


def invert_kernel(side_ref, pair_ref, own_ref, out_ref):
    rank = out_ref.shape[0]
    start = pair_ref.shape[2] - 2 * rank
    near = pair_ref[1 - side_ref[0], :, start:].astype(F32)
    gram = own_ref[...] + near[:, :rank] + near[:, rank:]
    rows = lax.broadcasted_iota(jnp.int32, (rank, 2 * rank), 0)
    lanes = lax.broadcasted_iota(jnp.int32, (rank, 2 * rank), 1)
    identity = (lanes - rank == rows).astype(F32)
    work = jnp.concatenate([gram, gram], axis=1)
    work = jnp.where(lanes < rank, work, identity)
    for start in range(0, rank, WIDE):
        top = start // 8 * 8
        active = work[top:]
        columns = [
            jnp.broadcast_to(active[:, start + i : start + i + 1], active.shape)
            for i in range(WIDE)
        ]
        for i in range(WIDE):
            row = start + i - top
            scale = 1.0 / columns[i][row : row + 1]
            below = jnp.where(rows[top:] > start + i, columns[i], 0.0)
            for j in range(i + 1, WIDE):
                across = columns[i][row + j - i : row + j - i + 1] * scale
                columns[j] = columns[j] - below * across
            active = active - below * (active[row : row + 1] * scale)
        work = active if top == 0 else jnp.concatenate([work[:top], active], axis=0)
    diagonal = jnp.sum(jnp.where(lanes == rows, work, 0.0), axis=1, keepdims=True)
    out_ref[...] = (work * lax.rsqrt(diagonal))[:, rank:]


def finish_kernel(gathered_ref, inverse_ref, out_ref):
    members, _, width = gathered_ref.shape
    cores = out_ref.shape[1] // width
    for core in range(cores):
        total = gathered_ref[core].astype(F32)
        for member in range(core + cores, members, cores):
            total += gathered_ref[member].astype(F32)
        out_ref[:, core * width : (core + 1) * width] = jnp.dot(
            inverse_ref[...], total * (1.0 / members), precision=HIGHEST, preferred_element_type=F32
        )


def input_grad_kernel(side_ref, grads_ref, grads_near_ref, weight_ref, out_ref):
    step, side = pl.program_id(0), side_ref[0]
    half = weight_ref.shape[0] // 2
    own = weight_ref[(1 - side) * half + half - 1 - step]
    near = weight_ref[side * half + step]
    total = dot(grads_ref[...], own, 1, 1) + dot(grads_near_ref[...], near, 1, 1)
    out_ref[...] = total.astype(BF16)


def input_grad(side, grads, grads_near, weight):
    tokens, _ = grads.shape
    pieces, rows, _ = weight.shape
    vmem = pl.BlockSpec(memory_space=pltpu.VMEM)
    return pl.pallas_call(
        input_grad_kernel,
        out_shape=jax.ShapeDtypeStruct((tokens, pieces // 2 * rows), BF16),
        grid=(pieces // 2,),
        in_specs=[pl.BlockSpec(memory_space=pltpu.SMEM), vmem, vmem, vmem],
        out_specs=pl.BlockSpec((tokens, rows), lambda step: (0, step)),
        cost_estimate=pl.CostEstimate(flops=10**9, bytes_accessed=3 * 10**6, transcendentals=0),
        compiler_params=pltpu.CompilerParams(vmem_limit_bytes=VMEM_LIMIT),
        name="input_grad",
    )(side, grads, grads_near, weight)


def weight_route(chips, cores, sections):
    def index(z, c, s, t):
        return ((z * cores + c) * sections + s) * 2 + t

    route = []
    for s in range(sections - 1):
        for z in range(chips):
            for c in range(cores):
                for t in range(2):
                    if z // (chips // 2) == t:
                        source = index(z, c, s + 1, 1 - t)
                    else:
                        source = index(chips - 1 - z, c, s + 1, t)
                    route.append((source, index(z, c, s, t)))
    return route


def on_device(activations, key_grads, key_weight, error_buf, q_prev):
    chips, cores, sections = (lax.axis_size(name) for name in ("z", "c", "pp"))
    groups = chips * cores
    side, core = place("tp"), place("c")
    inputs, grads, weight, error = activations[0], key_grads[0], key_weight[0], error_buf[0, 0]
    rank = q_prev.shape[2]
    tokens, features = inputs.shape
    columns = grads.shape[1]
    part = features // groups

    def shape(*sizes, kind=F32):
        return jax.ShapeDtypeStruct(sizes, kind)

    weight_piece = lax.ppermute(
        weight, ("z", "c", "pp", "tp"), weight_route(chips, cores, sections)
    )

    q_rows = q_prev[0].T
    payload = project(side, q_rows, grads, error)
    payload = lax.all_gather(payload, "tp", axis=0, tiled=False)
    payload, weight_piece = lax.optimization_barrier((payload, weight_piece))
    weight_all = lax.all_gather(weight_piece, GROUP, axis=0, tiled=False)
    factor = call(
        lambda *refs: left_kernel(groups, *refs),
        shape(cores, rank, features, kind=BF16),
        "left",
        (side, payload, q_rows, error, inputs),
    )
    factor = lax.all_to_all(factor, "c", 0, 0)
    shares = call(
        chip_sum_kernel,
        shape(groups, rank, part, kind=BF16),
        "chip_sum",
        (factor,),
        scalars=0,
    )
    shares, error_later = lax.optimization_barrier((shares, error))
    shares = lax.all_to_all(shares, GROUP, 0, 0)
    error_near = swap(
        lax.dynamic_slice_in_dim(error_later, (1 - side[0]) * features, features, 0), "tp"
    )
    spread = call(
        share_kernel, shape(groups, rank, part, kind=BF16), "share", (shares,), scalars=0
    )
    spread, grads_later = lax.optimization_barrier((spread, grads))
    factor = lax.all_to_all(spread, GROUP, 0, 0)
    grads_next = lax.ppermute(grads_later, "pp", [(i, i - 1) for i in range(1, sections)])
    grads_next_near = lax.ppermute(
        grads_later,
        ("pp", "tp"),
        [(2 * s + 2 + 1 - t, 2 * s + t) for s in range(sections - 1) for t in range(2)],
    )
    factor = lax.all_gather(factor, "c", axis=0, tiled=False)

    away, projected, coeffs, gram = call(
        right_kernel,
        (
            shape(rank, tokens + columns + 2 * rank, kind=BF16),
            shape(rank, tokens),
            shape(rank, columns),
            shape(rank, rank),
        ),
        "right",
        (side, factor, inputs, error_near, error),
    )
    pair = lax.all_gather(away, "tp", axis=0, tiled=False)
    pair, grads_next, grads_next_near = lax.optimization_barrier(
        (pair, grads_next, grads_next_near)
    )
    coeffs = call(
        join_kernel,
        shape(rank, columns, kind=BF16),
        "join",
        (side, pair, projected, coeffs, grads),
    )
    coeffs = lax.all_gather(coeffs, "c", axis=0, tiled=False)
    spread = call(
        spread_kernel, shape(groups, rank, columns // cores, kind=BF16), "spread", (core, coeffs)
    )
    gathered = lax.all_to_all(spread, GROUP, 0, 0)
    inverse = call(invert_kernel, shape(rank, rank), "invert", (side, pair, gram))
    grad_prev = input_grad(
        side, grads_next, grads_next_near, weight_all.reshape(chips, cores * tokens, columns)
    )
    gathered, inverse, grad_prev = lax.optimization_barrier((gathered, inverse, grad_prev))
    coeffs = call(finish_kernel, shape(rank, columns), "finish", (gathered, inverse), scalars=0)
    return (grad_prev[None], coeffs.T[None])


def solution(mesh):
    groups, sections, sides = (mesh.shape[name] for name in ("dp", "pp", "tp"))
    split_mesh = Mesh(
        mesh.devices.reshape(groups // 2, 2, sections, sides), ("z", "c", "pp", "tp")
    )
    return jax.shard_map(
        on_device,
        mesh=split_mesh,
        in_specs=(
            P("pp", GROUP, "tp"),
            P("pp", GROUP, "tp"),
            P("pp", GROUP, "tp"),
            P("pp", GROUP, None, "tp"),
            P("pp", "tp", None),
        ),
        out_specs=(P("pp", GROUP, "tp"), P("pp", "tp", None)),
        check_vma=False,
    )
```

time: 308 us -> 114 us (0.37)
  waiting for transfers between devices: 140 us -> 21 us
  blocking collectives: 112 us -> 32.8 us
  starting transfers between devices: 5.5 us -> 25.1 us
  matrix products: 17.8 us -> 0 us
  Pallas kernels: 0 us -> 13.5 us
  other arithmetic: 12.7 us -> 0 us
    psum x2 -> x0, blocking collectives: 90.3 us -> none  [the longest x1 45.7 us: on_device(): lax.psum(jnp.dot(factor_rows.T, factor_rows, precision=HIGHEST), 'dp')]
    all_gather x2 -> x1, waiting for transfers between devices: 83.8 us -> 0.01 us  [on_device(): weight_all = lax.all_gather(weight_piece, GROUP, axis=0, tiled=False)]
    reduce_scatter x2 -> x0, waiting for transfers between devices: 54.5 us -> none  [the longest x1 54.5 us: on_device(): lax.psum_scatter(factor.astype(jnp.bfloat16), 'dp', scatter_dimension=0,...]
    all_to_all x0 -> x3, waiting for transfers between devices: none -> 21 us  [the longest x1 10.9 us: on_device(): shares = lax.all_to_all(shares, GROUP, 0, 0)]
    dot_general x5 -> x0, matrix products: 16.7 us -> none  [the longest x1 4.98 us: on_device(): factor = jnp.dot(summed, coeffs_prev, precision=HIGHEST)]
    pallas_call x0 -> x10, Pallas kernels: none -> 13.5 us  [the longest x8 8.48 us: call(): pl.pallas_call(kernel, out_shape=out_shapes, in_specs=[pl.BlockSpec(memor...]
    another operation x5 -> x0, other arithmetic: 12.1 us -> none  [the longest x3 6.52 us: orthonormal(): lower_factor = jnp.linalg.cholesky(gram_matrix)]
    all_to_all x0 -> x3, starting transfers between devices: none -> 11.6 us  [the longest x1 4.09 us: on_device(): factor = lax.all_to_all(spread, GROUP, 0, 0)]
  transfers between devices with their start and end apart: 5 -> 8, of which waited for: 3 -> 3; matrix products, arithmetic and copies ran while one was open for 10% -> 1% of each run, Pallas kernels for 0% -> 11%
where the time goes in v2:
time: 114 us; the launch traced here: 112 us
  blocking collectives  32.8 us (29%)
  starting transfers between devices  25.1 us (22%)
  waiting for transfers between devices  21 us (18%)
  between operations  14.2 us (12%)
  Pallas kernels  13.5 us (12%)
  local copies, waits for them, and re-layouts  5.15 us (5%)
    all_gather x1, blocking collectives, on_device(): payload = lax.all_gather(payload, 'tp', axis=0, tiled=False)  18.1 us
    all_to_all x1, waiting for transfers between devices, on_device(): shares = lax.all_to_all(shares, GROUP, 0, 0)  10.9 us
    pallas_call x8, Pallas kernels, call(): pl.pallas_call(kernel, out_shape=out_shapes, in_specs=[pl.BlockSpec(memor...  8.48 us
    all_to_all x1, waiting for transfers between devices, on_device(): factor = lax.all_to_all(spread, GROUP, 0, 0)  5.6 us
    all_to_all x1, blocking collectives, on_device(): factor = lax.all_to_all(factor, 'c', 0, 0)  5.33 us
    ppermute x1, starting transfers between devices, on_device(): lax.ppermute(weight, ('z', 'c', 'pp', 'tp'), weight_route(chips, cores, s...  5.27 us
    all_to_all x1, waiting for transfers between devices, on_device(): gathered = lax.all_to_all(spread, GROUP, 0, 0)  4.51 us
    ppermute x1, starting transfers between devices, on_device(): lax.ppermute(grads_later, 'pp', [(i, i - 1) for i in range(1, sections)])  4.33 us
  transfers between devices with their start and end apart: 8, of which 3 were waited for; matrix products, arithmetic and copies ran while one was open for 1% of the time, Pallas kernels for 11%

profile of v2, /device:TPU:7, one launch (start us, length us, event | category | flops | bytes accessed | tf_op | source)
XLA Modules:
  0.0 111.8 jit_solution(2474092948366218834)
XLA Ops:
  7.2 0.0 all-gather.7.cloned.1.call-start
  7.2 5.3 %collective-permute-start = (bf16[256,256]{1,0:T(8,128)(2,1)}, bf16[256,256]{1,0:T(8,128)(2,1)S(1)}, u32[]{:S(2)}, u32[]{:S(2)}) collective-permute-start(bf16[256,256]{1,0:T(8,128)(2,1)} %bitcast.36), channel_id=1, source_target_pairs={{3,0},{451,1},{35,32},{483,33},{67,64},{387,65},{99,96},{419,97},{... | collective-permute-start | bytes 393224 | tf_op jit(solution)/shard_map/ppermute | solution.py:279
  12.5 2.6 %project.1 = bf16[64,2304]{1,0:T(8,128)(2,1)} custom-call(s32[1]{0:T(128)} %bitcast.1.side_ref.refs_0_, f32[64,256]{1,0:T(8,128)} %bitcast.32, bf16[256,256]{1,0:T(8,128)(2,1)} %bitcast.28, bf16[4096,256]{1,0:T(8,128)(2,1)} %bitcast.18), custom_call_target="tpu_custom_call" | custom-call | flops 100000000 | bytes 2000000 | tf_op jit(solution)/shard_map/project/pallas_call | solution.py:79
  15.1 18.1 %all-gather = bf16[128,2304]{1,0:T(8,128)(2,1)} all-gather(bf16[64,2304]{1,0:T(8,128)(2,1)} %project.1), channel_id=2, replica_groups=mesh['z'=8,'c'=2,'pp'=16,'tp'=2] {'tp'}, dimensions={0}, use_global_device_ids=true | all-gather | bytes 884736 | tf_op jit(solution)/shard_map/all_gather | solution.py:285
  33.2 0.7 copy-done.8
  33.9 0.0 all-gather.7.cloned.1.call-update
  34.0 1.1 copy-done.2
  35.0 0.7 left.1
  35.7 5.3 %all_to_all.20.pair_ref = bf16[2,64,2048]{2,1,0:T(8,128)(2,1)S(1)} all-to-all(bf16[2,64,2048]{2,1,0:T(8,128)(2,1)S(1)} %left.1), channel_id=1, replica_groups=mesh['z'=8,'c'=2,'pp'=16,'tp'=2] {'c'}, dimensions={0} | all-to-all | bytes 1048576 | tf_op jit(solution)/shard_map/all_to_all | solution.py:294
  41.0 0.8 chip_sum.1
  41.8 3.7 %all-to-all-start.1 = ((bf16[16,64,128]{2,1,0:T(8,128)(2,1)}), bf16[16,64,128]{2,1,0:T(8,128)(2,1)S(1)}, u32[]{:S(2)}, u32[]{:S(2)}) async-start(bf16[16,64,128]{2,1,0:T(8,128)(2,1)} %chip_sum.1), calls=%async_computation.1 | async-start | bytes 524288 | tf_op jit(solution)/shard_map/all_to_all | solution.py:303
  45.5 1.0 constant_dynamic-slice_fusion
  46.5 1.9 %collective-permute-start.1 = (bf16[2048,256]{1,0:T(8,128)(2,1)}, bf16[2048,256]{1,0:T(8,128)(2,1)}, u32[]{:S(2)}, u32[]{:S(2)}) collective-permute-start(bf16[2048,256]{1,0:T(8,128)(2,1)} %constant_dynamic-slice_fusion), channel_id=1, source_target_pairs={{0,1},{1,0},{2,3},{3,2},{4,5},{5,4},{6,7},{7,6},{8,9},{9,8},{10,11... | collective-permute-start | bytes 3145736 | tf_op jit(solution)/shard_map/ppermute | solution.py:20
  48.4 10.9 %all-to-all-done.1.shares_ref = bf16[16,64,128]{2,1,0:T(8,128)(2,1)S(1)} async-done(((bf16[16,64,128]{2,1,0:T(8,128)(2,1)}), bf16[16,64,128]{2,1,0:T(8,128)(2,1)S(1)}, u32[]{:S(2)}, u32[]{:S(2)}) %all-to-all-start.1) | async-done | bytes 262176 | tf_op jit(solution)/shard_map/all_to_all | solution.py:303
  59.3 0.7 share.1
  60.0 4.1 %all-to-all-start.2 = ((bf16[16,64,128]{2,1,0:T(8,128)(2,1)}), bf16[16,64,128]{2,1,0:T(8,128)(2,1)}, u32[]{:S(2)}, u32[]{:S(2)}) async-start(bf16[16,64,128]{2,1,0:T(8,128)(2,1)} %share.1), calls=%async_computation.2 | async-start | bytes 524288 | tf_op jit(solution)/shard_map/all_to_all | solution.py:311
  64.1 4.3 %collective-permute-start.2 = (bf16[256,256]{1,0:T(8,128)(2,1)S(1)}, bf16[256,256]{1,0:T(8,128)(2,1)S(1)}, u32[]{:S(2)}, u32[]{:S(2)}) collective-permute-start(bf16[256,256]{1,0:T(8,128)(2,1)S(1)} %bitcast.29), channel_id=1, source_target_pairs={{2,0},{4,2},{6,4},{8,6},{10,8},{12,10},{14,12},{16,14},{18,16},{20... | collective-permute-start | bytes 393224 | tf_op jit(solution)/shard_map/ppermute | solution.py:312
  68.5 1.9 %collective-permute-start.3 = (bf16[256,256]{1,0:T(8,128)(2,1)S(1)}, bf16[256,256]{1,0:T(8,128)(2,1)S(1)}, u32[]{:S(2)}, u32[]{:S(2)}) collective-permute-start(bf16[256,256]{1,0:T(8,128)(2,1)S(1)} %bitcast.30), channel_id=1, source_target_pairs={{3,0},{2,1},{5,2},{4,3},{7,4},{6,5},{9,6},{8,7},{11,8},{10,9},{13,... | collective-permute-start | bytes 393224 | tf_op jit(solution)/shard_map/ppermute | solution.py:313
  70.4 5.6 %all-to-all-done.2 = bf16[16,64,128]{2,1,0:T(8,128)(2,1)} async-done(((bf16[16,64,128]{2,1,0:T(8,128)(2,1)}), bf16[16,64,128]{2,1,0:T(8,128)(2,1)}, u32[]{:S(2)}, u32[]{:S(2)}) %all-to-all-start.2) | async-done | bytes 262176 | tf_op jit(solution)/shard_map/all_to_all | solution.py:311
  76.0 2.4 %all-gather.1 = bf16[32,64,128]{2,1,0:T(8,128)(2,1)S(1)} all-gather(bf16[16,64,128]{2,1,0:T(8,128)(2,1)} %all-to-all-done.2), channel_id=3, replica_groups=mesh['z'=8,'c'=2,'pp'=16,'tp'=2] {'c'}, dimensions={0}, use_global_device_ids=true | all-gather | bytes 786432 | tf_op jit(solution)/shard_map/all_gather | solution.py:318
  78.4 2.2 %right.1 = (bf16[64,640]{1,0:T(8,128)(2,1)S(1)}, f32[64,256]{1,0:T(8,128)S(1)}, f32[64,256]{1,0:T(8,128)S(1)}, f32[64,64]{1,0:T(8,128)S(1)}) custom-call(s32[1]{0:T(128)} %bitcast.1.side_ref.refs_0_, bf16[2,16,64,128]{3,2,1,0:T(8,128)(2,1)S(1)} %bitcast.25, bf16[256,2048]{1,0:T(8,128)(2,1)S(1)} %bitcast.23, ...), custom_call_target="tpu_custom_call" | custom-call | flops 100000000 | bytes 4000000 | tf_op jit(solution)/shard_map/right/pallas_call | solution.py:38
  80.6 4.3 %all-gather.2 = bf16[128,640]{1,0:T(8,128)(2,1)S(1)} all-gather(bf16[64,640]{1,0:T(8,128)(2,1)S(1)} %get-tuple-element.22), channel_id=4, replica_groups=mesh['z'=8,'c'=2,'pp'=16,'tp'=2] {'tp'}, dimensions={0}, use_global_device_ids=true | all-gather | bytes 245760 | tf_op jit(solution)/shard_map/all_gather | solution.py:331
  84.9 0.2 join.1
  85.1 2.7 %all-gather.3 = bf16[128,256]{1,0:T(8,128)(2,1)S(1)} all-gather(bf16[64,256]{1,0:T(8,128)(2,1)S(1)} %join.1), channel_id=5, replica_groups=mesh['z'=8,'c'=2,'pp'=16,'tp'=2] {'c'}, dimensions={0}, use_global_device_ids=true | all-gather | bytes 98304 | tf_op jit(solution)/shard_map/all_gather | solution.py:341
  87.8 0.7 spread.1
  88.5 3.8 %all-to-all-start.3 = ((bf16[16,64,128]{2,1,0:T(8,128)(2,1)}), bf16[16,64,128]{2,1,0:T(8,128)(2,1)S(1)}, u32[]{:S(2)}, u32[]{:S(2)}) async-start(bf16[16,64,128]{2,1,0:T(8,128)(2,1)} %spread.1), calls=%async_computation.3 | async-start | bytes 524288 | tf_op jit(solution)/shard_map/all_to_all | solution.py:345
  92.4 0.8 copy-done.7
  93.1 2.4 %invert.1.inverse_ref = f32[64,64]{1,0:T(8,128)S(1)} custom-call(s32[1]{0:T(128)} %bitcast.1.side_ref.refs_0_, bf16[2,64,640]{2,1,0:T(8,128)(2,1)S(1)} %bitcast.27, f32[64,64]{1,0:T(8,128)S(1)} %copy-done.7), custom_call_target="tpu_custom_call" | custom-call | flops 100000000 | bytes 4000000 | tf_op jit(solution)/shard_map/invert/pallas_call | solution.py:38
  95.5 1.6 %copy-done.5 = bf16[4096,256]{1,0:T(8,128)(2,1)S(1)} copy-done((bf16[4096,256]{1,0:T(8,128)(2,1)S(1)}, bf16[4096,256]{1,0:T(8,128)(2,1)}, u32[]{:S(2)}) %copy-start.5) | copy-done | bytes 2097176
  97.1 2.4 %input_grad.1 = bf16[256,2048]{1,0:T(8,128)(2,1)} custom-call(s32[1]{0:T(128)} %bitcast.1.side_ref.refs_0_, bf16[256,256]{1,0:T(8,128)(2,1)S(1)} %collective-permute-done.2.grads_ref, bf16[256,256]{1,0:T(8,128)(2,1)S(1)} %collective-permute-done.3.grads_near_ref, bf16[8,512,256]{2,1,0:T(8,128)(2,1)S(1)} %bitcast.35), custom_call_target="tpu_custom_call" | custom-call | flops 1000000000 | bytes 3000000 | tf_op jit(solution)/shard_map/input_grad/pallas_call | solution.py:237
  99.6 4.5 %all-to-all-done.3.gathered_ref = bf16[16,64,128]{2,1,0:T(8,128)(2,1)S(1)} async-done(((bf16[16,64,128]{2,1,0:T(8,128)(2,1)}), bf16[16,64,128]{2,1,0:T(8,128)(2,1)S(1)}, u32[]{:S(2)}, u32[]{:S(2)}) %all-to-all-start.3) | async-done | bytes 262176 | tf_op jit(solution)/shard_map/all_to_all | solution.py:345
  104.1 0.9 finish.1
  (19 shorter events, 0.0 us)
Async XLA Ops:
  7.2 26.8 %copy-start.4 = (f32[1,256,64]{1,2,0:T(8,128)S(1)}, f32[1,256,64]{1,2,0:T(8,128)}, u32[]{:S(2)}) copy-start(f32[1,256,64]{1,2,0:T(8,128)} %param.9) | copy-start | bytes 196612
  7.2 26.8 %copy-start = (bf16[1,1,4096,256]{3,2,1,0:T(8,128)(2,1)S(1)}, bf16[1,1,4096,256]{3,2,1,0:T(8,128)(2,1)}, u32[]{:S(2)}) copy-start(bf16[1,1,4096,256]{3,2,1,0:T(8,128)(2,1)} %param.8) | copy-start | bytes 6291460
  7.2 26.8 %copy-start.1 = (bf16[1,256,2048]{2,1,0:T(8,128)(2,1)S(1)}, bf16[1,256,2048]{2,1,0:T(8,128)(2,1)}, u32[]{:S(2)}) copy-start(bf16[1,256,2048]{2,1,0:T(8,128)(2,1)} %param.5) | copy-start | bytes 3145732
  7.2 88.3 %all-gather.7.cloned.1.call-start = ((), (), s32[]{:S(2)}) async-start(), calls=%async_computation.4 | async-start | bytes 2228224 | tf_op jit(solution)/shard_map/all_gather | solution.py:287
  7.2 26.0 %collective-permute-start = (bf16[256,256]{1,0:T(8,128)(2,1)}, bf16[256,256]{1,0:T(8,128)(2,1)S(1)}, u32[]{:S(2)}, u32[]{:S(2)}) collective-permute-start(bf16[256,256]{1,0:T(8,128)(2,1)} %bitcast.36), channel_id=1, source_target_pairs={{3,0},{451,1},{35,32},{483,33},{67,64},{387,65},{99,96},{419,97},{... | collective-permute-start | bytes 393224 | tf_op jit(solution)/shard_map/ppermute | solution.py:279
  33.2 0.7 copy-start.8
  33.9 1.1 copy-start.2
  41.0 23.1 %copy-start.3 = (bf16[1,256,256]{2,1,0:T(8,128)(2,1)S(1)}, bf16[1,256,256]{2,1,0:T(8,128)(2,1)}, u32[]{:S(2)}) copy-start(bf16[1,256,256]{2,1,0:T(8,128)(2,1)} %param.6) | copy-start | bytes 393220
  41.8 17.5 %all-to-all-start.1 = ((bf16[16,64,128]{2,1,0:T(8,128)(2,1)}), bf16[16,64,128]{2,1,0:T(8,128)(2,1)S(1)}, u32[]{:S(2)}, u32[]{:S(2)}) async-start(bf16[16,64,128]{2,1,0:T(8,128)(2,1)} %chip_sum.1), calls=%async_computation.1 | async-start | bytes 524288 | tf_op jit(solution)/shard_map/all_to_all | solution.py:303
  46.5 31.9 %collective-permute-start.1 = (bf16[2048,256]{1,0:T(8,128)(2,1)}, bf16[2048,256]{1,0:T(8,128)(2,1)}, u32[]{:S(2)}, u32[]{:S(2)}) collective-permute-start(bf16[2048,256]{1,0:T(8,128)(2,1)} %constant_dynamic-slice_fusion), channel_id=1, source_target_pairs={{0,1},{1,0},{2,3},{3,2},{4,5},{5,4},{6,7},{7,6},{8,9},{9,8},{10,11... | collective-permute-start | bytes 3145736 | tf_op jit(solution)/shard_map/ppermute | solution.py:20
  60.0 16.0 %all-to-all-start.2 = ((bf16[16,64,128]{2,1,0:T(8,128)(2,1)}), bf16[16,64,128]{2,1,0:T(8,128)(2,1)}, u32[]{:S(2)}, u32[]{:S(2)}) async-start(bf16[16,64,128]{2,1,0:T(8,128)(2,1)} %share.1), calls=%async_computation.2 | async-start | bytes 524288 | tf_op jit(solution)/shard_map/all_to_all | solution.py:311
  64.1 20.8 %collective-permute-start.2 = (bf16[256,256]{1,0:T(8,128)(2,1)S(1)}, bf16[256,256]{1,0:T(8,128)(2,1)S(1)}, u32[]{:S(2)}, u32[]{:S(2)}) collective-permute-start(bf16[256,256]{1,0:T(8,128)(2,1)S(1)} %bitcast.29), channel_id=1, source_target_pairs={{2,0},{4,2},{6,4},{8,6},{10,8},{12,10},{14,12},{16,14},{18,16},{20... | collective-permute-start | bytes 393224 | tf_op jit(solution)/shard_map/ppermute | solution.py:312
  68.5 16.5 %collective-permute-start.3 = (bf16[256,256]{1,0:T(8,128)(2,1)S(1)}, bf16[256,256]{1,0:T(8,128)(2,1)S(1)}, u32[]{:S(2)}, u32[]{:S(2)}) collective-permute-start(bf16[256,256]{1,0:T(8,128)(2,1)S(1)} %bitcast.30), channel_id=1, source_target_pairs={{3,0},{2,1},{5,2},{4,3},{7,4},{6,5},{9,6},{8,7},{11,8},{10,9},{13,... | collective-permute-start | bytes 393224 | tf_op jit(solution)/shard_map/ppermute | solution.py:313
  80.6 7.2 %copy-start.6 = (f32[64,64]{1,0:T(8,128)}, f32[64,64]{1,0:T(8,128)S(1)}, u32[]{:S(2)}) copy-start(f32[64,64]{1,0:T(8,128)S(1)} %get-tuple-element.27.own_ref) | copy-start | bytes 49156
  88.5 15.6 %all-to-all-start.3 = ((bf16[16,64,128]{2,1,0:T(8,128)(2,1)}), bf16[16,64,128]{2,1,0:T(8,128)(2,1)S(1)}, u32[]{:S(2)}, u32[]{:S(2)}) async-start(bf16[16,64,128]{2,1,0:T(8,128)(2,1)} %spread.1), calls=%async_computation.3 | async-start | bytes 524288 | tf_op jit(solution)/shard_map/all_to_all | solution.py:345
  92.4 0.8 copy-start.7
  95.5 1.6 %copy-start.5 = (bf16[4096,256]{1,0:T(8,128)(2,1)S(1)}, bf16[4096,256]{1,0:T(8,128)(2,1)}, u32[]{:S(2)}) copy-start(bf16[4096,256]{1,0:T(8,128)(2,1)} %all-gather.7.cloned.1.call-done) | copy-start | bytes 6291460
Sparse Core Ops, SparseCore 0:
  34.0 42.5 all-gather.6

commit v3 on v2

--- a/solution.py
+++ b/solution.py
@@ -118,56 +118,60 @@
 
 
 def share_kernel(shares_ref, out_ref):
-    groups = shares_ref.shape[0]
+    groups, rank, _ = shares_ref.shape
     for core in range(2):
         total = shares_ref[core].astype(F32)
         for member in range(core + 2, groups, 2):
             total += shares_ref[member].astype(F32)
-        total = total.astype(BF16)
-        for member in range(core, groups, 2):
-            out_ref[member] = total
-
-
-def right_kernel(
-    side_ref, factor_ref, inputs_ref, near_ref, error_ref, away_ref, projected_ref, own_ref, gram_ref
+        out_ref[core * rank : (core + 1) * rank] = total.astype(BF16)
+
+
+def two_chunks(factor_ref, chunk, rows):
+    return jnp.concatenate([factor_ref[chunk, rows], factor_ref[chunk + 1, rows]], axis=1)
+
+
+def right_kernel(core_ref, factor_ref, inputs_ref, away_ref, projected_ref, gram_ref):
+    chunks, both, width = factor_ref.shape
+    rank, half = both // 2, chunks // 2
+    tokens = inputs_ref.shape[0]
+    projected = jnp.zeros((both, tokens), F32)
+    gram = jnp.zeros((both, both), F32)
+    for chunk in range(0, chunks, 2):
+        factor = two_chunks(factor_ref, chunk, slice(None))
+        projected += dot(factor, inputs_ref[:, chunk * width : (chunk + 2) * width], 1, 1)
+        gram += dot(factor, factor, 1, 1)
+    for chunk in range(half):
+        lanes = slice(chunk * width, (chunk + 1) * width)
+        away_ref[:, lanes] = factor_ref[core_ref[0] * half + chunk, rank:]
+    start = half * width
+    away_ref[:, start : start + tokens] = projected[rank:].astype(BF16)
+    away_ref[:, start + tokens :] = split(gram[rank:, rank:], 1)
+    projected_ref[...] = projected[:rank]
+    gram_ref[...] = gram[:rank, :rank]
+
+
+def join_kernel(
+    side_ref, core_ref, pair_ref, factor_ref, projected_ref, grads_ref, error_ref, error_pair_ref,
+    out_ref,
 ):
-    _, chunks, rank, width = factor_ref.shape
+    chunks, both, width = factor_ref.shape
+    rank, tokens = both // 2, grads_ref.shape[0]
+    features, part = chunks * width, error_pair_ref.shape[0]
     side = side_ref[0]
-    tokens, features = inputs_ref.shape
-    columns = own_ref.shape[1]
-    projected = jnp.zeros((2 * rank, tokens), F32)
-    gram = jnp.zeros((2 * rank, 2 * rank), F32)
-    own = jnp.zeros((rank, columns), F32)
-    near = jnp.zeros((rank, columns), F32)
-    for chunk in range(0, chunks, 2):
-        factor = jnp.concatenate(
-            [
-                jnp.concatenate([factor_ref[block, chunk + i] for i in range(2)], axis=1)
-                for block in range(2)
-            ],
-            axis=0,
-        )
-        lanes = slice(chunk * width, (chunk + 2) * width)
-        projected += dot(factor, inputs_ref[:, lanes], 1, 1)
-        gram += dot(factor, factor, 1, 1)
-        near += dot(factor[rank:], near_ref[lanes])
-        start, size = chunk * width, 2 * width
+    near_ref = pair_ref.at[1 - side]
+    near = near_ref[:, part : part + tokens].astype(F32)
+    total = dot((projected_ref[...] + near).astype(BF16), grads_ref[...])
+    size = 2 * width
+    for start in range(0, features, size):
         rows = pl.ds(pl.multiple_of(side * features + start, size), size)
-        own += dot(factor[:rank], error_ref[rows])
-    away_ref[:, :tokens] = projected[rank:].astype(BF16)
-    away_ref[:, tokens : tokens + columns] = near.astype(BF16)
-    away_ref[:, tokens + columns :] = split(gram[rank:, rank:], 1)
-    projected_ref[...] = projected[:rank]
-    own_ref[...] = own
-    gram_ref[...] = gram[:rank, :rank]
-
-
-def join_kernel(side_ref, pair_ref, projected_ref, own_ref, grads_ref, out_ref):
-    tokens, columns = grads_ref.shape
-    near = pair_ref[1 - side_ref[0]].astype(F32)
-    projected = (projected_ref[...] + near[:, :tokens]).astype(BF16)
-    total = own_ref[...] + near[:, tokens : tokens + columns]
-    out_ref[...] = (total + dot(projected, grads_ref[...])).astype(BF16)
+        total += dot(two_chunks(factor_ref, start // width, slice(rank)), error_ref[rows])
+    for start in range(0, part, size):
+        lanes = slice(start, start + size)
+        first = (1 - side) * features + core_ref[0] * part + start
+        rows = pl.ds(pl.multiple_of(first, size), size)
+        total += dot(near_ref[:, lanes], error_ref[rows])
+        total += dot(near_ref[:, lanes], error_pair_ref[lanes])
+    out_ref[...] = total.astype(BF16)
 
 
 def spread_kernel(core_ref, pair_ref, out_ref):
@@ -299,44 +303,40 @@
         (factor,),
         scalars=0,
     )
-    shares, error_later = lax.optimization_barrier((shares, error))
+    shares, error_later, grads_later = lax.optimization_barrier((shares, error, grads))
     shares = lax.all_to_all(shares, GROUP, 0, 0)
-    error_near = swap(
-        lax.dynamic_slice_in_dim(error_later, (1 - side[0]) * features, features, 0), "tp"
-    )
-    spread = call(
-        share_kernel, shape(groups, rank, part, kind=BF16), "share", (shares,), scalars=0
-    )
-    spread, grads_later = lax.optimization_barrier((spread, grads))
-    factor = lax.all_to_all(spread, GROUP, 0, 0)
     grads_next = lax.ppermute(grads_later, "pp", [(i, i - 1) for i in range(1, sections)])
     grads_next_near = lax.ppermute(
         grads_later,
         ("pp", "tp"),
         [(2 * s + 2 + 1 - t, 2 * s + t) for s in range(sections - 1) for t in range(2)],
     )
-    factor = lax.all_gather(factor, "c", axis=0, tiled=False)
-
-    away, projected, coeffs, gram = call(
+    error_part = features // cores
+    error_away = (1 - side[0]) * features + (1 - core[0]) * error_part
+    error_pair = swap(lax.dynamic_slice_in_dim(error_later, error_away, error_part, 0), "c")
+    share = call(share_kernel, shape(2 * rank, part, kind=BF16), "share", (shares,), scalars=0)
+    factor = lax.all_gather(share, GROUP, axis=0, tiled=False)
+    factor, grads_next, grads_next_near, error_pair = lax.optimization_barrier(
+        (factor, grads_next, grads_next_near, error_pair)
+    )
+
+    away, projected, gram = call(
         right_kernel,
         (
-            shape(rank, tokens + columns + 2 * rank, kind=BF16),
+            shape(rank, error_part + tokens + 2 * rank, kind=BF16),
             shape(rank, tokens),
-            shape(rank, columns),
             shape(rank, rank),
         ),
         "right",
-        (side, factor, inputs, error_near, error),
+        (core, factor, inputs),
     )
     pair = lax.all_gather(away, "tp", axis=0, tiled=False)
-    pair, grads_next, grads_next_near = lax.optimization_barrier(
-        (pair, grads_next, grads_next_near)
-    )
     coeffs = call(
         join_kernel,
         shape(rank, columns, kind=BF16),
         "join",
-        (side, pair, projected, coeffs, grads),
+        (side, core, pair, factor, projected, grads, error, error_pair),
+        scalars=2,
     )
     coeffs = lax.all_gather(coeffs, "c", axis=0, tiled=False)
     spread = call(

time: 114 us -> 113 us (level); the launches traced: 112 us -> 113 us
  blocking collectives: 32.8 us -> 49.2 us
  waiting for transfers between devices: 21 us -> 9.49 us
  starting transfers between devices: 25.1 us -> 22 us
    all_gather x1, blocking collectives: 2.4 us -> 16.5 us  [on_device(): factor = lax.all_gather(share, GROUP, axis=0, tiled=False)]
    all_to_all x1, waiting for transfers between devices: 10.9 us -> 5.16 us  [on_device(): shares = lax.all_to_all(shares, GROUP, 0, 0)]
    all_to_all x1 -> x0, waiting for transfers between devices: 5.6 us -> none  [on_device(): factor = lax.all_to_all(spread, GROUP, 0, 0)]
    all_to_all x1 -> x0, starting transfers between devices: 4.09 us -> none  [on_device(): factor = lax.all_to_all(spread, GROUP, 0, 0)]
    all_gather x1, blocking collectives: 4.33 us -> 6.67 us  [on_device(): pair = lax.all_gather(away, 'tp', axis=0, tiled=False)]
    all_to_all x1, starting transfers between devices: 3.84 us -> 5.39 us  [on_device(): gathered = lax.all_to_all(spread, GROUP, 0, 0)]
    unnamed x18 -> x14, local copies, waits for them, and re-layouts: 4.11 us -> 3.34 us
  transfers between devices with their start and end apart: 8 -> 7, of which waited for: 3 -> 2; matrix products, arithmetic and copies ran while one was open for 1% -> 1% of each run, Pallas kernels for 11% -> 11%
where the time goes in v3:
time: 113 us
  blocking collectives  49.2 us (44%)
  starting transfers between devices  22 us (19%)
  between operations  14.2 us (13%)
  Pallas kernels  13.7 us (12%)
  waiting for transfers between devices  9.49 us (8%)
  local copies, waits for them, and re-layouts  4.16 us (4%)
    all_gather x1, blocking collectives, on_device(): payload = lax.all_gather(payload, 'tp', axis=0, tiled=False)  18.1 us
    all_gather x1, blocking collectives, on_device(): factor = lax.all_gather(share, GROUP, axis=0, tiled=False)  16.5 us
    pallas_call x8, Pallas kernels, call(): pl.pallas_call(kernel, out_shape=out_shapes, in_specs=[pl.BlockSpec(memor...  7.69 us
    all_gather x1, blocking collectives, on_device(): pair = lax.all_gather(away, 'tp', axis=0, tiled=False)  6.67 us
    all_to_all x1, blocking collectives, on_device(): factor = lax.all_to_all(factor, 'c', 0, 0)  5.46 us
    all_to_all x1, starting transfers between devices, on_device(): gathered = lax.all_to_all(spread, GROUP, 0, 0)  5.39 us
    ppermute x1, starting transfers between devices, on_device(): lax.ppermute(weight, ('z', 'c', 'pp', 'tp'), weight_route(chips, cores, s...  5.27 us
    all_to_all x1, waiting for transfers between devices, on_device(): shares = lax.all_to_all(shares, GROUP, 0, 0)  5.16 us
  transfers between devices with their start and end apart: 7, of which 2 were waited for; matrix products, arithmetic and copies ran while one was open for 1% of the time, Pallas kernels for 11%

profile of v3, /device:TPU:7, one launch (start us, length us, event | category | flops | bytes accessed | tf_op | source)
XLA Modules:
  0.0 112.7 jit_solution(14091060706188114371)
XLA Ops:
  7.2 0.0 all-gather.7.cloned.1.call-start
  7.2 5.3 %collective-permute-start = (bf16[256,256]{1,0:T(8,128)(2,1)}, bf16[256,256]{1,0:T(8,128)(2,1)S(1)}, u32[]{:S(2)}, u32[]{:S(2)}) collective-permute-start(bf16[256,256]{1,0:T(8,128)(2,1)} %bitcast.37), channel_id=1, source_target_pairs={{3,0},{451,1},{35,32},{483,33},{67,64},{387,65},{99,96},{419,97},{... | collective-permute-start | bytes 393224 | tf_op jit(solution)/shard_map/ppermute | solution.py:283
  12.5 2.6 %project.1 = bf16[64,2304]{1,0:T(8,128)(2,1)} custom-call(s32[1]{0:T(128)} %bitcast.1.side_ref.refs_0_, f32[64,256]{1,0:T(8,128)} %bitcast.33, bf16[256,256]{1,0:T(8,128)(2,1)} %bitcast.29, bf16[4096,256]{1,0:T(8,128)(2,1)} %bitcast.18), custom_call_target="tpu_custom_call" | custom-call | flops 100000000 | bytes 2000000 | tf_op jit(solution)/shard_map/project/pallas_call | solution.py:79
  15.1 18.1 %all-gather = bf16[128,2304]{1,0:T(8,128)(2,1)} all-gather(bf16[64,2304]{1,0:T(8,128)(2,1)} %project.1), channel_id=2, replica_groups=mesh['z'=8,'c'=2,'pp'=16,'tp'=2] {'tp'}, dimensions={0}, use_global_device_ids=true | all-gather | bytes 884736 | tf_op jit(solution)/shard_map/all_gather | solution.py:289
  33.2 0.0 collective-permute-done
  33.2 0.6 copy-done.6
  33.9 0.0 all-gather.7.cloned.1.call-update
  33.9 1.1 copy-done.2
  35.0 0.7 left.1
  35.6 0.0 copy-start.3
  35.7 5.5 %all_to_all.15.pair_ref = bf16[2,64,2048]{2,1,0:T(8,128)(2,1)S(1)} all-to-all(bf16[2,64,2048]{2,1,0:T(8,128)(2,1)S(1)} %left.1), channel_id=1, replica_groups=mesh['z'=8,'c'=2,'pp'=16,'tp'=2] {'c'}, dimensions={0} | all-to-all | bytes 1048576 | tf_op jit(solution)/shard_map/all_to_all | solution.py:298
  41.1 0.8 chip_sum.1
  41.9 3.7 %all-to-all-start.1 = ((bf16[16,64,128]{2,1,0:T(8,128)(2,1)}), bf16[16,64,128]{2,1,0:T(8,128)(2,1)S(1)}, u32[]{:S(2)}, u32[]{:S(2)}) async-start(bf16[16,64,128]{2,1,0:T(8,128)(2,1)} %chip_sum.1), calls=%async_computation.1 | async-start | bytes 524288 | tf_op jit(solution)/shard_map/all_to_all | solution.py:307
  45.6 0.8 constant_dynamic-slice_fusion
  46.4 2.1 %collective-permute-start.3 = (bf16[1024,256]{1,0:T(8,128)(2,1)}, bf16[1024,256]{1,0:T(8,128)(2,1)}, u32[]{:S(2)}, u32[]{:S(2)}) collective-permute-start(bf16[1024,256]{1,0:T(8,128)(2,1)} %constant_dynamic-slice_fusion), channel_id=1, source_target_pairs={{0,32},{32,0},{1,33},{33,1},{2,34},{34,2},{3,35},{35,3},{4,36},{36... | collective-permute-start | bytes 1572872 | tf_op jit(solution)/shard_map/ppermute | solution.py:20
  48.6 3.6 %collective-permute-start.1 = (bf16[256,256]{1,0:T(8,128)(2,1)S(1)}, bf16[256,256]{1,0:T(8,128)(2,1)}, u32[]{:S(2)}, u32[]{:S(2)}) collective-permute-start(bf16[256,256]{1,0:T(8,128)(2,1)S(1)} %bitcast.30), channel_id=1, source_target_pairs={{2,0},{4,2},{6,4},{8,6},{10,8},{12,10},{14,12},{16,14},{18,16},{20... | collective-permute-start | bytes 393224 | tf_op jit(solution)/shard_map/ppermute | solution.py:308
  52.2 1.9 %collective-permute-start.2 = (bf16[256,256]{1,0:T(8,128)(2,1)S(1)}, bf16[256,256]{1,0:T(8,128)(2,1)}, u32[]{:S(2)}, u32[]{:S(2)}) collective-permute-start(bf16[256,256]{1,0:T(8,128)(2,1)S(1)} %bitcast.31), channel_id=1, source_target_pairs={{3,0},{2,1},{5,2},{4,3},{7,4},{6,5},{9,6},{8,7},{11,8},{10,9},{13,... | collective-permute-start | bytes 393224 | tf_op jit(solution)/shard_map/ppermute | solution.py:309
  54.1 5.2 %all-to-all-done.1.shares_ref = bf16[16,64,128]{2,1,0:T(8,128)(2,1)S(1)} async-done(((bf16[16,64,128]{2,1,0:T(8,128)(2,1)}), bf16[16,64,128]{2,1,0:T(8,128)(2,1)S(1)}, u32[]{:S(2)}, u32[]{:S(2)}) %all-to-all-start.1) | async-done | bytes 262176 | tf_op jit(solution)/shard_map/all_to_all | solution.py:307
  59.3 16.5 %all-gather.1 = bf16[2048,128]{1,0:T(8,128)(2,1)S(1)} all-gather(bf16[128,128]{1,0:T(8,128)(2,1)S(1)} %share.1), channel_id=3, replica_groups=mesh['z'=8,'c'=2,'pp'=16,'tp'=2] {'z','c'}, dimensions={0}, use_global_device_ids=true | all-gather | bytes 557056 | tf_op jit(solution)/shard_map/all_gather | solution.py:318
  75.8 0.0 collective-permute-done.1.grads_ref
  75.8 0.0 collective-permute-done.2.grads_near_ref
  75.8 0.7 right.1
  76.5 6.7 %all-gather.2 = bf16[128,1408]{1,0:T(8,128)(2,1)S(1)} all-gather(bf16[64,1408]{1,0:T(8,128)(2,1)S(1)} %get-tuple-element.22), channel_id=4, replica_groups=mesh['z'=8,'c'=2,'pp'=16,'tp'=2] {'tp'}, dimensions={0}, use_global_device_ids=true | all-gather | bytes 540672 | tf_op jit(solution)/shard_map/all_gather | solution.py:333
  83.2 1.6 %join.1 = bf16[64,256]{1,0:T(8,128)(2,1)S(1)} custom-call(s32[1]{0:T(128)} %bitcast.1.side_ref.refs_0_, s32[1]{0:T(128)} %bitcast.core_ref, bf16[2,64,1408]{2,1,0:T(8,128)(2,1)S(1)} %bitcast.26, bf16[16,128,128]{2,1,0:T(8,128)(2,1)S(1)} %bitcast.23, f32[64,256]{1,0:T(8,128)S(1)} %get-tuple-element.23.projected_ref, bf16[256,256]{1,0:T(8,128)(2,1)S(1)} %bitcast.32, ...), custom_call_target="tpu_custom_call" | custom-call | flops 100000000 | bytes 4000000 | tf_op jit(solution)/shard_map/join/pallas_call | solution.py:38
  84.7 2.5 %all-gather.3 = bf16[128,256]{1,0:T(8,128)(2,1)S(1)} all-gather(bf16[64,256]{1,0:T(8,128)(2,1)S(1)} %join.1), channel_id=5, replica_groups=mesh['z'=8,'c'=2,'pp'=16,'tp'=2] {'c'}, dimensions={0}, use_global_device_ids=true | all-gather | bytes 98304 | tf_op jit(solution)/shard_map/all_gather | solution.py:341
  87.2 0.7 spread.1
  87.9 5.4 %all-to-all-start.2 = ((bf16[16,64,128]{2,1,0:T(8,128)(2,1)}), bf16[16,64,128]{2,1,0:T(8,128)(2,1)S(1)}, u32[]{:S(2)}, u32[]{:S(2)}) async-start(bf16[16,64,128]{2,1,0:T(8,128)(2,1)} %spread.1), calls=%async_computation.2 | async-start | bytes 524288 | tf_op jit(solution)/shard_map/all_to_all | solution.py:345
  93.3 2.4 %invert.1.inverse_ref = f32[64,64]{1,0:T(8,128)S(1)} custom-call(s32[1]{0:T(128)} %bitcast.1.side_ref.refs_0_, bf16[2,64,1408]{2,1,0:T(8,128)(2,1)S(1)} %bitcast.27, f32[64,64]{1,0:T(8,128)S(1)} %get-tuple-element.25.own_ref), custom_call_target="tpu_custom_call" | custom-call | flops 100000000 | bytes 4000000 | tf_op jit(solution)/shard_map/invert/pallas_call | solution.py:38
  95.7 1.6 %copy-done.5 = bf16[4096,256]{1,0:T(8,128)(2,1)S(1)} copy-done((bf16[4096,256]{1,0:T(8,128)(2,1)S(1)}, bf16[4096,256]{1,0:T(8,128)(2,1)}, u32[]{:S(2)}) %copy-start.5) | copy-done | bytes 2097176
  97.3 3.4 %input_grad.1 = bf16[256,2048]{1,0:T(8,128)(2,1)} custom-call(s32[1]{0:T(128)} %bitcast.1.side_ref.refs_0_, bf16[256,256]{1,0:T(8,128)(2,1)} %collective-permute-done.1.grads_ref, bf16[256,256]{1,0:T(8,128)(2,1)} %collective-permute-done.2.grads_near_ref, bf16[8,512,256]{2,1,0:T(8,128)(2,1)S(1)} %bitcast.36), custom_call_target="tpu_custom_call" | custom-call | flops 1000000000 | bytes 3000000 | tf_op jit(solution)/shard_map/input_grad/pallas_call | solution.py:241
  100.7 4.3 %all-to-all-done.2.gathered_ref = bf16[16,64,128]{2,1,0:T(8,128)(2,1)S(1)} async-done(((bf16[16,64,128]{2,1,0:T(8,128)(2,1)}), bf16[16,64,128]{2,1,0:T(8,128)(2,1)S(1)}, u32[]{:S(2)}, u32[]{:S(2)}) %all-to-all-start.2) | async-done | bytes 262176 | tf_op jit(solution)/shard_map/all_to_all | solution.py:345
  105.0 0.9 finish.1
  (13 shorter events, 0.1 us)
Async XLA Ops:
  7.2 26.7 %copy-start.4 = (f32[1,256,64]{1,2,0:T(8,128)S(1)}, f32[1,256,64]{1,2,0:T(8,128)}, u32[]{:S(2)}) copy-start(f32[1,256,64]{1,2,0:T(8,128)} %param.9) | copy-start | bytes 196612
  7.2 26.7 %copy-start = (bf16[1,1,4096,256]{3,2,1,0:T(8,128)(2,1)S(1)}, bf16[1,1,4096,256]{3,2,1,0:T(8,128)(2,1)}, u32[]{:S(2)}) copy-start(bf16[1,1,4096,256]{3,2,1,0:T(8,128)(2,1)} %param.8) | copy-start | bytes 6291460
  7.2 26.7 %copy-start.1 = (bf16[1,256,2048]{2,1,0:T(8,128)(2,1)S(1)}, bf16[1,256,2048]{2,1,0:T(8,128)(2,1)}, u32[]{:S(2)}) copy-start(bf16[1,256,2048]{2,1,0:T(8,128)(2,1)} %param.5) | copy-start | bytes 3145732
  7.2 88.5 %all-gather.7.cloned.1.call-start = ((), (), s32[]{:S(2)}) async-start(), calls=%async_computation.3 | async-start | bytes 2228224 | tf_op jit(solution)/shard_map/all_gather | solution.py:291
  7.2 26.0 %collective-permute-start = (bf16[256,256]{1,0:T(8,128)(2,1)}, bf16[256,256]{1,0:T(8,128)(2,1)S(1)}, u32[]{:S(2)}, u32[]{:S(2)}) collective-permute-start(bf16[256,256]{1,0:T(8,128)(2,1)} %bitcast.37), channel_id=1, source_target_pairs={{3,0},{451,1},{35,32},{483,33},{67,64},{387,65},{99,96},{419,97},{... | collective-permute-start | bytes 393224 | tf_op jit(solution)/shard_map/ppermute | solution.py:283
  33.2 0.6 copy-start.6
  33.9 1.1 copy-start.2
  35.6 12.9 %copy-start.3 = (bf16[1,256,256]{2,1,0:T(8,128)(2,1)S(1)}, bf16[1,256,256]{2,1,0:T(8,128)(2,1)}, u32[]{:S(2)}) copy-start(bf16[1,256,256]{2,1,0:T(8,128)(2,1)} %param.6) | copy-start | bytes 393220
  41.9 17.4 %all-to-all-start.1 = ((bf16[16,64,128]{2,1,0:T(8,128)(2,1)}), bf16[16,64,128]{2,1,0:T(8,128)(2,1)S(1)}, u32[]{:S(2)}, u32[]{:S(2)}) async-start(bf16[16,64,128]{2,1,0:T(8,128)(2,1)} %chip_sum.1), calls=%async_computation.1 | async-start | bytes 524288 | tf_op jit(solution)/shard_map/all_to_all | solution.py:307
  46.4 29.4 %collective-permute-start.3 = (bf16[1024,256]{1,0:T(8,128)(2,1)}, bf16[1024,256]{1,0:T(8,128)(2,1)}, u32[]{:S(2)}, u32[]{:S(2)}) collective-permute-start(bf16[1024,256]{1,0:T(8,128)(2,1)} %constant_dynamic-slice_fusion), channel_id=1, source_target_pairs={{0,32},{32,0},{1,33},{33,1},{2,34},{34,2},{3,35},{35,3},{4,36},{36... | collective-permute-start | bytes 1572872 | tf_op jit(solution)/shard_map/ppermute | solution.py:20
  48.6 27.2 %collective-permute-start.1 = (bf16[256,256]{1,0:T(8,128)(2,1)S(1)}, bf16[256,256]{1,0:T(8,128)(2,1)}, u32[]{:S(2)}, u32[]{:S(2)}) collective-permute-start(bf16[256,256]{1,0:T(8,128)(2,1)S(1)} %bitcast.30), channel_id=1, source_target_pairs={{2,0},{4,2},{6,4},{8,6},{10,8},{12,10},{14,12},{16,14},{18,16},{20... | collective-permute-start | bytes 393224 | tf_op jit(solution)/shard_map/ppermute | solution.py:308
  52.2 23.6 %collective-permute-start.2 = (bf16[256,256]{1,0:T(8,128)(2,1)S(1)}, bf16[256,256]{1,0:T(8,128)(2,1)}, u32[]{:S(2)}, u32[]{:S(2)}) collective-permute-start(bf16[256,256]{1,0:T(8,128)(2,1)S(1)} %bitcast.31), channel_id=1, source_target_pairs={{3,0},{2,1},{5,2},{4,3},{7,4},{6,5},{9,6},{8,7},{11,8},{10,9},{13,... | collective-permute-start | bytes 393224 | tf_op jit(solution)/shard_map/ppermute | solution.py:309
  87.9 17.1 %all-to-all-start.2 = ((bf16[16,64,128]{2,1,0:T(8,128)(2,1)}), bf16[16,64,128]{2,1,0:T(8,128)(2,1)S(1)}, u32[]{:S(2)}, u32[]{:S(2)}) async-start(bf16[16,64,128]{2,1,0:T(8,128)(2,1)} %spread.1), calls=%async_computation.2 | async-start | bytes 524288 | tf_op jit(solution)/shard_map/all_to_all | solution.py:345
  95.7 1.6 %copy-start.5 = (bf16[4096,256]{1,0:T(8,128)(2,1)S(1)}, bf16[4096,256]{1,0:T(8,128)(2,1)}, u32[]{:S(2)}) copy-start(bf16[4096,256]{1,0:T(8,128)(2,1)} %all-gather.7.cloned.1.call-done) | copy-start | bytes 6291460
Sparse Core Ops, SparseCore 0:
  34.0 40.3 all-gather.6

commit v4 on v3

--- a/solution.py
+++ b/solution.py
@@ -52,59 +52,69 @@
 
 
 def project_kernel(
-    side_ref, q_hbm, grads_hbm, error_hbm, payload_ref, q_ref, grads_ref, error_ref, arrived
+    side_ref, core_ref, q_hbm, grads_hbm, error_hbm, pair_hbm, payload_ref,
+    q_ref, grads_ref, error_ref, arrived,
 ):
-    features, tokens = error_ref.shape[0], grads_ref.shape[0]
-    away = pl.ds(pl.multiple_of((1 - side_ref[0]) * features, features), features)
-    sources = (q_hbm, grads_hbm, error_hbm.at[away])
-    targets = (q_ref, grads_ref, error_ref)
-    copies = [pltpu.make_async_copy(*sources_targets, arrived.at[i])
-              for i, sources_targets in enumerate(zip(sources, targets))]
+    part = pair_hbm.shape[0]
+    features = error_hbm.shape[0] // 2
+    first = (1 - side_ref[0]) * features + core_ref[0] * part
+    sources = (q_hbm, grads_hbm, error_hbm.at[pl.ds(pl.multiple_of(first, part), part)], pair_hbm)
+    targets = (q_ref, grads_ref, error_ref.at[0], error_ref.at[1])
+    copies = [
+        pltpu.make_async_copy(source, target, arrived.at[i])
+        for i, (source, target) in enumerate(zip(sources, targets))
+    ]
     for copy in copies:
         copy.start()
     copies[0].wait()
     q_parts = split(q_ref[...], 0)
     copies[1].wait()
-    payload_ref[:, features:] = times_q(q_parts, grads_ref[...]).astype(BF16)
+    payload_ref[:, part:] = times_q(q_parts, grads_ref[...]).astype(BF16)
     copies[2].wait()
-    for start in range(0, features, STEP):
+    copies[3].wait()
+    for start in range(0, part, STEP):
         rows = slice(start, start + STEP)
-        payload_ref[:, rows] = times_q(q_parts, error_ref[rows]).astype(BF16)
-
-
-def project(side, q_prev, grads, error):
+        total = times_q(q_parts, error_ref[0, rows]) + times_q(q_parts, error_ref[1, rows])
+        payload_ref[:, rows] = total.astype(BF16)
+
+
+def project(side, core, q_prev, grads, error, error_pair):
     rank, columns = q_prev.shape
-    tokens, features = grads.shape[0], error.shape[0] // 2
+    tokens, part = grads.shape[0], error_pair.shape[0]
+    smem = pl.BlockSpec(memory_space=pltpu.SMEM)
     hbm = pl.BlockSpec(memory_space=pltpu.HBM)
     return pl.pallas_call(
         project_kernel,
-        out_shape=jax.ShapeDtypeStruct((rank, features + tokens), BF16),
-        in_specs=[pl.BlockSpec(memory_space=pltpu.SMEM), hbm, hbm, hbm],
+        out_shape=jax.ShapeDtypeStruct((rank, part + tokens), BF16),
+        in_specs=[smem, smem, hbm, hbm, hbm, hbm],
         out_specs=pl.BlockSpec(memory_space=pltpu.VMEM),
         scratch_shapes=[
             pltpu.VMEM((rank, columns), F32),
             pltpu.VMEM((tokens, columns), BF16),
-            pltpu.VMEM((features, columns), BF16),
-            pltpu.SemaphoreType.DMA((3,)),
+            pltpu.VMEM((2, part, columns), BF16),
+            pltpu.SemaphoreType.DMA((4,)),
         ],
         cost_estimate=pl.CostEstimate(flops=10**8, bytes_accessed=2 * 10**6, transcendentals=0),
         compiler_params=pltpu.CompilerParams(vmem_limit_bytes=VMEM_ALL),
         name="project",
-    )(side, q_prev, grads, error)
-
-
-def left_kernel(groups, side_ref, pair_ref, q_ref, error_ref, inputs_ref, out_ref):
+    )(side, core, q_prev, grads, error, error_pair)
+
+
+def left_kernel(groups, side_ref, core_ref, pair_ref, q_ref, error_ref, inputs_ref, out_ref):
     features, side = inputs_ref.shape[1], side_ref[0]
     rank = q_ref.shape[0]
     payload_ref, near_ref = pair_ref.at[side], pair_ref.at[1 - side]
     q_parts = split(q_ref[...], 0)
-    mixed = jnp.concatenate([payload_ref[:, features:], near_ref[:, features:]], axis=0)
+    part = payload_ref.shape[1] - inputs_ref.shape[0]
+    mixed = jnp.concatenate([payload_ref[:, part:], near_ref[:, part:]], axis=0)
     for start in range(0, features, STEP):
         lanes = slice(start, start + STEP)
         rows = pl.ds(pl.multiple_of(side * features + start, STEP), STEP)
         product = dot(mixed, inputs_ref[:, lanes])
         own = (product[:rank] + times_q(q_parts, error_ref[rows])) * (1.0 / groups)
-        near = (product[rank:] + near_ref[:, lanes].astype(F32)) * (1.0 / groups)
+        carried = near_ref[:, start % part : start % part + STEP].astype(F32)
+        carried = jnp.where(core_ref[0] == start // part, carried, 0.0)
+        near = (product[rank:] + carried) * (1.0 / groups)
         out_ref[0, :, lanes] = own.astype(BF16)
         out_ref[1, :, lanes] = near.astype(BF16)
 
@@ -284,8 +294,12 @@
         weight, ("z", "c", "pp", "tp"), weight_route(chips, cores, sections)
     )
 
+    error_part = features // cores
+    error_away = (1 - side[0]) * features + (1 - core[0]) * error_part
+    error_pair = swap(lax.dynamic_slice_in_dim(error, error_away, error_part, 0), "c")
+
     q_rows = q_prev[0].T
-    payload = project(side, q_rows, grads, error)
+    payload = project(side, core, q_rows, grads, error, error_pair)
     payload = lax.all_gather(payload, "tp", axis=0, tiled=False)
     payload, weight_piece = lax.optimization_barrier((payload, weight_piece))
     weight_all = lax.all_gather(weight_piece, GROUP, axis=0, tiled=False)
@@ -293,7 +307,8 @@
         lambda *refs: left_kernel(groups, *refs),
         shape(cores, rank, features, kind=BF16),
         "left",
-        (side, payload, q_rows, error, inputs),
+        (side, core, payload, q_rows, error, inputs),
+        scalars=2,
     )
     factor = lax.all_to_all(factor, "c", 0, 0)
     shares = call(
@@ -303,7 +318,7 @@
         (factor,),
         scalars=0,
     )
-    shares, error_later, grads_later = lax.optimization_barrier((shares, error, grads))
+    shares, grads_later = lax.optimization_barrier((shares, grads))
     shares = lax.all_to_all(shares, GROUP, 0, 0)
     grads_next = lax.ppermute(grads_later, "pp", [(i, i - 1) for i in range(1, sections)])
     grads_next_near = lax.ppermute(
@@ -311,13 +326,10 @@
         ("pp", "tp"),
         [(2 * s + 2 + 1 - t, 2 * s + t) for s in range(sections - 1) for t in range(2)],
     )
-    error_part = features // cores
-    error_away = (1 - side[0]) * features + (1 - core[0]) * error_part
-    error_pair = swap(lax.dynamic_slice_in_dim(error_later, error_away, error_part, 0), "c")
     share = call(share_kernel, shape(2 * rank, part, kind=BF16), "share", (shares,), scalars=0)
     factor = lax.all_gather(share, GROUP, axis=0, tiled=False)
-    factor, grads_next, grads_next_near, error_pair = lax.optimization_barrier(
-        (factor, grads_next, grads_next_near, error_pair)
+    factor, grads_next, grads_next_near = lax.optimization_barrier(
+        (factor, grads_next, grads_next_near)
     )
 
     away, projected, gram = call(

time: 113 us -> 112 us (level); the launches traced: 113 us -> 110 us
  blocking collectives: 49.2 us -> 45.9 us
  starting transfers between devices: 22 us -> 23.2 us
    all_gather x1, blocking collectives: 18.1 us -> 14.3 us  [on_device(): payload = lax.all_gather(payload, 'tp', axis=0, tiled=False)]
    ppermute x1, starting transfers between devices: 1.92 us -> 4.53 us  [on_device(): lax.ppermute(grads_later, ('pp', 'tp'), [(2 * s + 2 + 1 - t, 2 * s + t) f...]
    all_to_all x1, starting transfers between devices: 5.39 us -> 3.8 us  [on_device(): gathered = lax.all_to_all(spread, GROUP, 0, 0)]
    all_gather x1, blocking collectives: 16.5 us -> 17.7 us  [on_device(): factor = lax.all_gather(share, GROUP, axis=0, tiled=False)]
  transfers between devices with their start and end apart: 7 -> 7, of which waited for: 2 -> 2; matrix products, arithmetic and copies ran while one was open for 1% -> 0% of each run, Pallas kernels for 11% -> 11%
where the time goes in v4:
time: 112 us; the launch traced here: 110 us
  blocking collectives  45.9 us (41%)
  starting transfers between devices  23.2 us (21%)
  between operations  14.2 us (13%)
  Pallas kernels  12.6 us (11%)
  waiting for transfers between devices  10.4 us (9%)
  local copies, waits for them, and re-layouts  3.66 us (3%)
    all_gather x1, blocking collectives, on_device(): factor = lax.all_gather(share, GROUP, axis=0, tiled=False)  17.7 us
    all_gather x1, blocking collectives, on_device(): payload = lax.all_gather(payload, 'tp', axis=0, tiled=False)  14.3 us
    all_gather x1, blocking collectives, on_device(): pair = lax.all_gather(away, 'tp', axis=0, tiled=False)  6.66 us
    pallas_call x8, Pallas kernels, call(): pl.pallas_call(kernel, out_shape=out_shapes, in_specs=[pl.BlockSpec(memor...  6.65 us
    all_to_all x1, waiting for transfers between devices, on_device(): shares = lax.all_to_all(shares, GROUP, 0, 0)  6.09 us
    ppermute x1, starting transfers between devices, on_device(): lax.ppermute(weight, ('z', 'c', 'pp', 'tp'), weight_route(chips, cores, s...  5.02 us
    all_to_all x1, blocking collectives, on_device(): factor = lax.all_to_all(factor, 'c', 0, 0)  4.7 us
    ppermute x1, starting transfers between devices, on_device(): lax.ppermute(grads_later, ('pp', 'tp'), [(2 * s + 2 + 1 - t, 2 * s + t) f...  4.53 us
  transfers between devices with their start and end apart: 7, of which 2 were waited for; matrix products, arithmetic and copies ran while one was open for 0% of the time, Pallas kernels for 11%

profile of v4, /device:TPU:7, one launch (start us, length us, event | category | flops | bytes accessed | tf_op | source)
XLA Modules:
  0.0 110.0 jit_solution(4522387548094059456)
XLA Ops:
  7.2 0.0 all-gather.7.cloned.1.call-start
  7.2 0.0 copy-start
  7.2 0.0 copy-start.5
  7.3 1.2 %dynamic-slice_bitcast_fusion = bf16[1024,256]{1,0:T(8,128)(2,1)S(1)} fusion(bf16[1,1,4096,256]{3,2,1,0:T(8,128)(2,1)} %param.8, s32[]{:T(128)S(6)} %select_n.3), kind=kLoop, calls=%fused_computation | loop fusion | bytes 1048580 | tf_op jit(solution)/shard_map/dynamic_slice | solution.py:299
  8.5 2.6 %collective-permute-start = (bf16[1024,256]{1,0:T(8,128)(2,1)S(1)}, bf16[1024,256]{1,0:T(8,128)(2,1)S(1)}, u32[]{:S(2)}, u32[]{:S(2)}) collective-permute-start(bf16[1024,256]{1,0:T(8,128)(2,1)S(1)} %dynamic-slice_bitcast_fusion), channel_id=1, source_target_pairs={{0,32},{32,0},{1,33},{33,1},{2,34},{34,2},{3,35},{35,3},{4,36},{36... | collective-permute-start | bytes 1572872 | tf_op jit(solution)/shard_map/ppermute | solution.py:20
  11.1 5.0 %collective-permute-start.1 = (bf16[256,256]{1,0:T(8,128)(2,1)}, bf16[256,256]{1,0:T(8,128)(2,1)}, u32[]{:S(2)}, u32[]{:S(2)}) collective-permute-start(bf16[256,256]{1,0:T(8,128)(2,1)} %bitcast.38), channel_id=1, source_target_pairs={{3,0},{451,1},{35,32},{483,33},{67,64},{387,65},{99,96},{419,97},{... | collective-permute-start | bytes 393224 | tf_op jit(solution)/shard_map/ppermute | solution.py:293
  16.1 0.0 copy-start.2
  16.1 0.8 copy-done.2
  16.9 2.5 %project.1 = bf16[64,1280]{1,0:T(8,128)(2,1)} custom-call(s32[1]{0:T(128)} %bitcast.1.side_ref.refs_0_, s32[1]{0:T(128)} %bitcast.core_ref.refs_1_, f32[64,256]{1,0:T(8,128)} %bitcast.34, bf16[256,256]{1,0:T(8,128)(2,1)} %bitcast.30, bf16[4096,256]{1,0:T(8,128)(2,1)} %bitcast.20, bf16[1024,256]{1,0:T(8,128)(2,1)} %copy-done.2), custom_call_target="tpu_custom_call" | custom-call | flops 100000000 | bytes 2000000 | tf_op jit(solution)/shard_map/project/pallas_call | solution.py:86
  19.5 14.3 %all-gather = bf16[128,1280]{1,0:T(8,128)(2,1)S(1)} all-gather(bf16[64,1280]{1,0:T(8,128)(2,1)} %project.1), channel_id=2, replica_groups=mesh['z'=8,'c'=2,'pp'=16,'tp'=2] {'tp'}, dimensions={0}, use_global_device_ids=true | all-gather | bytes 491520 | tf_op jit(solution)/shard_map/all_gather | solution.py:303
  33.8 0.0 collective-permute-done.1
  33.8 0.0 all-gather.7.cloned.1.call-update
  33.9 0.7 left.1
  34.5 0.0 copy-start.4
  34.5 4.7 %all_to_all.15.pair_ref = bf16[2,64,2048]{2,1,0:T(8,128)(2,1)S(1)} all-to-all(bf16[2,64,2048]{2,1,0:T(8,128)(2,1)S(1)} %left.1), channel_id=1, replica_groups=mesh['z'=8,'c'=2,'pp'=16,'tp'=2] {'c'}, dimensions={0} | all-to-all | bytes 1048576 | tf_op jit(solution)/shard_map/all_to_all | solution.py:313
  39.2 0.8 chip_sum.1
  40.0 3.7 %all-to-all-start.1 = ((bf16[16,64,128]{2,1,0:T(8,128)(2,1)}), bf16[16,64,128]{2,1,0:T(8,128)(2,1)S(1)}, u32[]{:S(2)}, u32[]{:S(2)}) async-start(bf16[16,64,128]{2,1,0:T(8,128)(2,1)} %chip_sum.1), calls=%async_computation.1 | async-start | bytes 524288 | tf_op jit(solution)/shard_map/all_to_all | solution.py:322
  43.7 3.6 %collective-permute-start.2 = (bf16[256,256]{1,0:T(8,128)(2,1)S(1)}, bf16[256,256]{1,0:T(8,128)(2,1)}, u32[]{:S(2)}, u32[]{:S(2)}) collective-permute-start(bf16[256,256]{1,0:T(8,128)(2,1)S(1)} %bitcast.31), channel_id=1, source_target_pairs={{2,0},{4,2},{6,4},{8,6},{10,8},{12,10},{14,12},{16,14},{18,16},{20... | collective-permute-start | bytes 393224 | tf_op jit(solution)/shard_map/ppermute | solution.py:323
  47.3 4.5 %collective-permute-start.3 = (bf16[256,256]{1,0:T(8,128)(2,1)S(1)}, bf16[256,256]{1,0:T(8,128)(2,1)}, u32[]{:S(2)}, u32[]{:S(2)}) collective-permute-start(bf16[256,256]{1,0:T(8,128)(2,1)S(1)} %bitcast.32), channel_id=1, source_target_pairs={{3,0},{2,1},{5,2},{4,3},{7,4},{6,5},{9,6},{8,7},{11,8},{10,9},{13,... | collective-permute-start | bytes 393224 | tf_op jit(solution)/shard_map/ppermute | solution.py:324
  51.8 6.1 %all-to-all-done.1.shares_ref = bf16[16,64,128]{2,1,0:T(8,128)(2,1)S(1)} async-done(((bf16[16,64,128]{2,1,0:T(8,128)(2,1)}), bf16[16,64,128]{2,1,0:T(8,128)(2,1)S(1)}, u32[]{:S(2)}, u32[]{:S(2)}) %all-to-all-start.1) | async-done | bytes 262176 | tf_op jit(solution)/shard_map/all_to_all | solution.py:322
  58.0 17.7 %all-gather.1 = bf16[2048,128]{1,0:T(8,128)(2,1)S(1)} all-gather(bf16[128,128]{1,0:T(8,128)(2,1)S(1)} %share.1), channel_id=3, replica_groups=mesh['z'=8,'c'=2,'pp'=16,'tp'=2] {'z','c'}, dimensions={0}, use_global_device_ids=true | all-gather | bytes 557056 | tf_op jit(solution)/shard_map/all_gather | solution.py:330
  75.7 0.7 right.1
  76.4 6.7 %all-gather.2 = bf16[128,1408]{1,0:T(8,128)(2,1)S(1)} all-gather(bf16[64,1408]{1,0:T(8,128)(2,1)S(1)} %get-tuple-element.19), channel_id=4, replica_groups=mesh['z'=8,'c'=2,'pp'=16,'tp'=2] {'tp'}, dimensions={0}, use_global_device_ids=true | all-gather | bytes 540672 | tf_op jit(solution)/shard_map/all_gather | solution.py:345
  83.0 0.5 join.1
  83.6 2.5 %all-gather.3 = bf16[128,256]{1,0:T(8,128)(2,1)S(1)} all-gather(bf16[64,256]{1,0:T(8,128)(2,1)S(1)} %join.1), channel_id=5, replica_groups=mesh['z'=8,'c'=2,'pp'=16,'tp'=2] {'c'}, dimensions={0}, use_global_device_ids=true | all-gather | bytes 98304 | tf_op jit(solution)/shard_map/all_gather | solution.py:353
  86.0 0.7 spread.1
  86.8 3.8 %all-to-all-start.2 = ((bf16[16,64,128]{2,1,0:T(8,128)(2,1)}), bf16[16,64,128]{2,1,0:T(8,128)(2,1)S(1)}, u32[]{:S(2)}, u32[]{:S(2)}) async-start(bf16[16,64,128]{2,1,0:T(8,128)(2,1)} %spread.1), calls=%async_computation.2 | async-start | bytes 524288 | tf_op jit(solution)/shard_map/all_to_all | solution.py:357
  90.6 2.4 %invert.1.inverse_ref = f32[64,64]{1,0:T(8,128)S(1)} custom-call(s32[1]{0:T(128)} %bitcast.1.side_ref.refs_0_, bf16[2,64,1408]{2,1,0:T(8,128)(2,1)S(1)} %bitcast.28, f32[64,64]{1,0:T(8,128)S(1)} %get-tuple-element.21.own_ref), custom_call_target="tpu_custom_call" | custom-call | flops 100000000 | bytes 4000000 | tf_op jit(solution)/shard_map/invert/pallas_call | solution.py:38
  93.0 1.6 %copy-done.6 = bf16[4096,256]{1,0:T(8,128)(2,1)S(1)} copy-done((bf16[4096,256]{1,0:T(8,128)(2,1)S(1)}, bf16[4096,256]{1,0:T(8,128)(2,1)}, u32[]{:S(2)}) %copy-start.6) | copy-done | bytes 2097176
  94.6 3.4 %input_grad.1 = bf16[256,2048]{1,0:T(8,128)(2,1)} custom-call(s32[1]{0:T(128)} %bitcast.1.side_ref.refs_0_, bf16[256,256]{1,0:T(8,128)(2,1)} %collective-permute-done.2.grads_ref, bf16[256,256]{1,0:T(8,128)(2,1)} %collective-permute-done.3.grads_near_ref, bf16[8,512,256]{2,1,0:T(8,128)(2,1)S(1)} %bitcast.37), custom_call_target="tpu_custom_call" | custom-call | flops 1000000000 | bytes 3000000 | tf_op jit(solution)/shard_map/input_grad/pallas_call | solution.py:251
  98.0 4.3 %all-to-all-done.2.gathered_ref = bf16[16,64,128]{2,1,0:T(8,128)(2,1)S(1)} async-done(((bf16[16,64,128]{2,1,0:T(8,128)(2,1)}), bf16[16,64,128]{2,1,0:T(8,128)(2,1)S(1)}, u32[]{:S(2)}, u32[]{:S(2)}) %all-to-all-start.2) | async-done | bytes 262176 | tf_op jit(solution)/shard_map/all_to_all | solution.py:357
  102.3 0.9 finish.1
  (13 shorter events, 0.1 us)
Async XLA Ops:
  7.2 85.8 %all-gather.7.cloned.1.call-start = ((), (), s32[]{:S(2)}) async-start(), calls=%async_computation.3 | async-start | bytes 2228224 | tf_op jit(solution)/shard_map/all_gather | solution.py:305
  7.2 26.6 %copy-start = (bf16[1,1,4096,256]{3,2,1,0:T(8,128)(2,1)S(1)}, bf16[1,1,4096,256]{3,2,1,0:T(8,128)(2,1)}, u32[]{:S(2)}) copy-start(bf16[1,1,4096,256]{3,2,1,0:T(8,128)(2,1)} %param.8) | copy-start | bytes 6291460
  7.2 26.6 %copy-start.1 = (bf16[1,256,2048]{2,1,0:T(8,128)(2,1)S(1)}, bf16[1,256,2048]{2,1,0:T(8,128)(2,1)}, u32[]{:S(2)}) copy-start(bf16[1,256,2048]{2,1,0:T(8,128)(2,1)} %param.5) | copy-start | bytes 3145732
  7.2 26.6 %copy-start.5 = (f32[1,256,64]{1,2,0:T(8,128)S(1)}, f32[1,256,64]{1,2,0:T(8,128)}, u32[]{:S(2)}) copy-start(f32[1,256,64]{1,2,0:T(8,128)} %param.9) | copy-start | bytes 196612
  8.5 7.6 %collective-permute-start = (bf16[1024,256]{1,0:T(8,128)(2,1)S(1)}, bf16[1024,256]{1,0:T(8,128)(2,1)S(1)}, u32[]{:S(2)}, u32[]{:S(2)}) collective-permute-start(bf16[1024,256]{1,0:T(8,128)(2,1)S(1)} %dynamic-slice_bitcast_fusion), channel_id=1, source_target_pairs={{0,32},{32,0},{1,33},{33,1},{2,34},{34,2},{3,35},{35,3},{4,36},{36... | collective-permute-start | bytes 1572872 | tf_op jit(solution)/shard_map/ppermute | solution.py:20
  11.1 22.7 %collective-permute-start.1 = (bf16[256,256]{1,0:T(8,128)(2,1)}, bf16[256,256]{1,0:T(8,128)(2,1)}, u32[]{:S(2)}, u32[]{:S(2)}) collective-permute-start(bf16[256,256]{1,0:T(8,128)(2,1)} %bitcast.38), channel_id=1, source_target_pairs={{3,0},{451,1},{35,32},{483,33},{67,64},{387,65},{99,96},{419,97},{... | collective-permute-start | bytes 393224 | tf_op jit(solution)/shard_map/ppermute | solution.py:293
  16.1 0.8 copy-start.2
  34.5 9.2 %copy-start.4 = (bf16[1,256,256]{2,1,0:T(8,128)(2,1)S(1)}, bf16[1,256,256]{2,1,0:T(8,128)(2,1)}, u32[]{:S(2)}) copy-start(bf16[1,256,256]{2,1,0:T(8,128)(2,1)} %param.6) | copy-start | bytes 393220
  40.0 17.9 %all-to-all-start.1 = ((bf16[16,64,128]{2,1,0:T(8,128)(2,1)}), bf16[16,64,128]{2,1,0:T(8,128)(2,1)S(1)}, u32[]{:S(2)}, u32[]{:S(2)}) async-start(bf16[16,64,128]{2,1,0:T(8,128)(2,1)} %chip_sum.1), calls=%async_computation.1 | async-start | bytes 524288 | tf_op jit(solution)/shard_map/all_to_all | solution.py:322
  43.7 32.0 %collective-permute-start.2 = (bf16[256,256]{1,0:T(8,128)(2,1)S(1)}, bf16[256,256]{1,0:T(8,128)(2,1)}, u32[]{:S(2)}, u32[]{:S(2)}) collective-permute-start(bf16[256,256]{1,0:T(8,128)(2,1)S(1)} %bitcast.31), channel_id=1, source_target_pairs={{2,0},{4,2},{6,4},{8,6},{10,8},{12,10},{14,12},{16,14},{18,16},{20... | collective-permute-start | bytes 393224 | tf_op jit(solution)/shard_map/ppermute | solution.py:323
  47.3 28.4 %collective-permute-start.3 = (bf16[256,256]{1,0:T(8,128)(2,1)S(1)}, bf16[256,256]{1,0:T(8,128)(2,1)}, u32[]{:S(2)}, u32[]{:S(2)}) collective-permute-start(bf16[256,256]{1,0:T(8,128)(2,1)S(1)} %bitcast.32), channel_id=1, source_target_pairs={{3,0},{2,1},{5,2},{4,3},{7,4},{6,5},{9,6},{8,7},{11,8},{10,9},{13,... | collective-permute-start | bytes 393224 | tf_op jit(solution)/shard_map/ppermute | solution.py:324
  57.9 25.1 %copy-start.3 = (bf16[1024,256]{1,0:T(8,128)(2,1)S(1)}, bf16[1024,256]{1,0:T(8,128)(2,1)}, u32[]{:S(2)}) copy-start(bf16[1024,256]{1,0:T(8,128)(2,1)} %copy-done.2) | copy-start | bytes 1572868
  86.8 15.5 %all-to-all-start.2 = ((bf16[16,64,128]{2,1,0:T(8,128)(2,1)}), bf16[16,64,128]{2,1,0:T(8,128)(2,1)S(1)}, u32[]{:S(2)}, u32[]{:S(2)}) async-start(bf16[16,64,128]{2,1,0:T(8,128)(2,1)} %spread.1), calls=%async_computation.2 | async-start | bytes 524288 | tf_op jit(solution)/shard_map/all_to_all | solution.py:357
  93.0 1.6 %copy-start.6 = (bf16[4096,256]{1,0:T(8,128)(2,1)S(1)}, bf16[4096,256]{1,0:T(8,128)(2,1)}, u32[]{:S(2)}) copy-start(bf16[4096,256]{1,0:T(8,128)(2,1)} %all-gather.7.cloned.1.call-done) | copy-start | bytes 6291460
Sparse Core Ops, SparseCore 0:
  33.9 41.9 all-gather.6

commit v5 on v4

--- a/solution.py
+++ b/solution.py
@@ -86,7 +86,7 @@
     return pl.pallas_call(
         project_kernel,
         out_shape=jax.ShapeDtypeStruct((rank, part + tokens), BF16),
-        in_specs=[smem, smem, hbm, hbm, hbm, hbm],
+        in_specs=[smem, smem, hbm, hbm, hbm, pl.BlockSpec(memory_space=pl.ANY)],
         out_specs=pl.BlockSpec(memory_space=pltpu.VMEM),
         scratch_shapes=[
             pltpu.VMEM((rank, columns), F32),

time: 112 us -> 112 us (level)
  no operation moved by 1% of the time
where the time goes in v5:
time: 112 us; the launch traced here: 110 us
  blocking collectives  45.9 us (41%)
  starting transfers between devices  23.2 us (21%)
  between operations  14.2 us (13%)
  Pallas kernels  12.6 us (11%)
  waiting for transfers between devices  10.4 us (9%)
  local copies, waits for them, and re-layouts  3.66 us (3%)
    all_gather x1, blocking collectives, on_device(): factor = lax.all_gather(share, GROUP, axis=0, tiled=False)  17.7 us
    all_gather x1, blocking collectives, on_device(): payload = lax.all_gather(payload, 'tp', axis=0, tiled=False)  14.3 us
    all_gather x1, blocking collectives, on_device(): pair = lax.all_gather(away, 'tp', axis=0, tiled=False)  6.66 us
    pallas_call x8, Pallas kernels, call(): pl.pallas_call(kernel, out_shape=out_shapes, in_specs=[pl.BlockSpec(memor...  6.65 us
    all_to_all x1, waiting for transfers between devices, on_device(): shares = lax.all_to_all(shares, GROUP, 0, 0)  6.09 us
    ppermute x1, starting transfers between devices, on_device(): lax.ppermute(weight, ('z', 'c', 'pp', 'tp'), weight_route(chips, cores, s...  5.02 us
    all_to_all x1, blocking collectives, on_device(): factor = lax.all_to_all(factor, 'c', 0, 0)  4.7 us
    ppermute x1, starting transfers between devices, on_device(): lax.ppermute(grads_later, ('pp', 'tp'), [(2 * s + 2 + 1 - t, 2 * s + t) f...  4.53 us
  transfers between devices with their start and end apart: 7, of which 2 were waited for; matrix products, arithmetic and copies ran while one was open for 0% of the time, Pallas kernels for 11%

profile of v5, /device:TPU:7, one launch (start us, length us, event | category | flops | bytes accessed | tf_op | source)
XLA Modules:
  0.0 110.0 jit_solution(4522387548094059456)
XLA Ops:
  7.2 0.0 all-gather.7.cloned.1.call-start
  7.2 0.0 copy-start
  7.2 0.0 copy-start.5
  7.3 1.2 %dynamic-slice_bitcast_fusion = bf16[1024,256]{1,0:T(8,128)(2,1)S(1)} fusion(bf16[1,1,4096,256]{3,2,1,0:T(8,128)(2,1)} %param.8, s32[]{:T(128)S(6)} %select_n.3), kind=kLoop, calls=%fused_computation | loop fusion | bytes 1048580 | tf_op jit(solution)/shard_map/dynamic_slice | solution.py:299
  8.5 2.6 %collective-permute-start = (bf16[1024,256]{1,0:T(8,128)(2,1)S(1)}, bf16[1024,256]{1,0:T(8,128)(2,1)S(1)}, u32[]{:S(2)}, u32[]{:S(2)}) collective-permute-start(bf16[1024,256]{1,0:T(8,128)(2,1)S(1)} %dynamic-slice_bitcast_fusion), channel_id=1, source_target_pairs={{0,32},{32,0},{1,33},{33,1},{2,34},{34,2},{3,35},{35,3},{4,36},{36... | collective-permute-start | bytes 1572872 | tf_op jit(solution)/shard_map/ppermute | solution.py:20
  11.1 5.0 %collective-permute-start.1 = (bf16[256,256]{1,0:T(8,128)(2,1)}, bf16[256,256]{1,0:T(8,128)(2,1)}, u32[]{:S(2)}, u32[]{:S(2)}) collective-permute-start(bf16[256,256]{1,0:T(8,128)(2,1)} %bitcast.38), channel_id=1, source_target_pairs={{3,0},{451,1},{35,32},{483,33},{67,64},{387,65},{99,96},{419,97},{... | collective-permute-start | bytes 393224 | tf_op jit(solution)/shard_map/ppermute | solution.py:293
  16.1 0.0 copy-start.2
  16.1 0.8 copy-done.2
  16.9 2.5 %project.1 = bf16[64,1280]{1,0:T(8,128)(2,1)} custom-call(s32[1]{0:T(128)} %bitcast.1.side_ref.refs_0_, s32[1]{0:T(128)} %bitcast.core_ref.refs_1_, f32[64,256]{1,0:T(8,128)} %bitcast.34, bf16[256,256]{1,0:T(8,128)(2,1)} %bitcast.30, bf16[4096,256]{1,0:T(8,128)(2,1)} %bitcast.20, bf16[1024,256]{1,0:T(8,128)(2,1)} %copy-done.2), custom_call_target="tpu_custom_call" | custom-call | flops 100000000 | bytes 2000000 | tf_op jit(solution)/shard_map/project/pallas_call | solution.py:86
  19.5 14.3 %all-gather = bf16[128,1280]{1,0:T(8,128)(2,1)S(1)} all-gather(bf16[64,1280]{1,0:T(8,128)(2,1)} %project.1), channel_id=2, replica_groups=mesh['z'=8,'c'=2,'pp'=16,'tp'=2] {'tp'}, dimensions={0}, use_global_device_ids=true | all-gather | bytes 491520 | tf_op jit(solution)/shard_map/all_gather | solution.py:303
  33.8 0.0 collective-permute-done.1
  33.8 0.0 all-gather.7.cloned.1.call-update
  33.9 0.7 left.1
  34.5 0.0 copy-start.4
  34.5 4.7 %all_to_all.15.pair_ref = bf16[2,64,2048]{2,1,0:T(8,128)(2,1)S(1)} all-to-all(bf16[2,64,2048]{2,1,0:T(8,128)(2,1)S(1)} %left.1), channel_id=1, replica_groups=mesh['z'=8,'c'=2,'pp'=16,'tp'=2] {'c'}, dimensions={0} | all-to-all | bytes 1048576 | tf_op jit(solution)/shard_map/all_to_all | solution.py:313
  39.2 0.8 chip_sum.1
  40.0 3.7 %all-to-all-start.1 = ((bf16[16,64,128]{2,1,0:T(8,128)(2,1)}), bf16[16,64,128]{2,1,0:T(8,128)(2,1)S(1)}, u32[]{:S(2)}, u32[]{:S(2)}) async-start(bf16[16,64,128]{2,1,0:T(8,128)(2,1)} %chip_sum.1), calls=%async_computation.1 | async-start | bytes 524288 | tf_op jit(solution)/shard_map/all_to_all | solution.py:322
  43.7 3.6 %collective-permute-start.2 = (bf16[256,256]{1,0:T(8,128)(2,1)S(1)}, bf16[256,256]{1,0:T(8,128)(2,1)}, u32[]{:S(2)}, u32[]{:S(2)}) collective-permute-start(bf16[256,256]{1,0:T(8,128)(2,1)S(1)} %bitcast.31), channel_id=1, source_target_pairs={{2,0},{4,2},{6,4},{8,6},{10,8},{12,10},{14,12},{16,14},{18,16},{20... | collective-permute-start | bytes 393224 | tf_op jit(solution)/shard_map/ppermute | solution.py:323
  47.3 4.5 %collective-permute-start.3 = (bf16[256,256]{1,0:T(8,128)(2,1)S(1)}, bf16[256,256]{1,0:T(8,128)(2,1)}, u32[]{:S(2)}, u32[]{:S(2)}) collective-permute-start(bf16[256,256]{1,0:T(8,128)(2,1)S(1)} %bitcast.32), channel_id=1, source_target_pairs={{3,0},{2,1},{5,2},{4,3},{7,4},{6,5},{9,6},{8,7},{11,8},{10,9},{13,... | collective-permute-start | bytes 393224 | tf_op jit(solution)/shard_map/ppermute | solution.py:324
  51.8 6.1 %all-to-all-done.1.shares_ref = bf16[16,64,128]{2,1,0:T(8,128)(2,1)S(1)} async-done(((bf16[16,64,128]{2,1,0:T(8,128)(2,1)}), bf16[16,64,128]{2,1,0:T(8,128)(2,1)S(1)}, u32[]{:S(2)}, u32[]{:S(2)}) %all-to-all-start.1) | async-done | bytes 262176 | tf_op jit(solution)/shard_map/all_to_all | solution.py:322
  58.0 17.7 %all-gather.1 = bf16[2048,128]{1,0:T(8,128)(2,1)S(1)} all-gather(bf16[128,128]{1,0:T(8,128)(2,1)S(1)} %share.1), channel_id=3, replica_groups=mesh['z'=8,'c'=2,'pp'=16,'tp'=2] {'z','c'}, dimensions={0}, use_global_device_ids=true | all-gather | bytes 557056 | tf_op jit(solution)/shard_map/all_gather | solution.py:330
  75.7 0.7 right.1
  76.4 6.7 %all-gather.2 = bf16[128,1408]{1,0:T(8,128)(2,1)S(1)} all-gather(bf16[64,1408]{1,0:T(8,128)(2,1)S(1)} %get-tuple-element.19), channel_id=4, replica_groups=mesh['z'=8,'c'=2,'pp'=16,'tp'=2] {'tp'}, dimensions={0}, use_global_device_ids=true | all-gather | bytes 540672 | tf_op jit(solution)/shard_map/all_gather | solution.py:345
  83.0 0.5 join.1
  83.6 2.5 %all-gather.3 = bf16[128,256]{1,0:T(8,128)(2,1)S(1)} all-gather(bf16[64,256]{1,0:T(8,128)(2,1)S(1)} %join.1), channel_id=5, replica_groups=mesh['z'=8,'c'=2,'pp'=16,'tp'=2] {'c'}, dimensions={0}, use_global_device_ids=true | all-gather | bytes 98304 | tf_op jit(solution)/shard_map/all_gather | solution.py:353
  86.0 0.7 spread.1
  86.8 3.8 %all-to-all-start.2 = ((bf16[16,64,128]{2,1,0:T(8,128)(2,1)}), bf16[16,64,128]{2,1,0:T(8,128)(2,1)S(1)}, u32[]{:S(2)}, u32[]{:S(2)}) async-start(bf16[16,64,128]{2,1,0:T(8,128)(2,1)} %spread.1), calls=%async_computation.2 | async-start | bytes 524288 | tf_op jit(solution)/shard_map/all_to_all | solution.py:357
  90.6 2.4 %invert.1.inverse_ref = f32[64,64]{1,0:T(8,128)S(1)} custom-call(s32[1]{0:T(128)} %bitcast.1.side_ref.refs_0_, bf16[2,64,1408]{2,1,0:T(8,128)(2,1)S(1)} %bitcast.28, f32[64,64]{1,0:T(8,128)S(1)} %get-tuple-element.21.own_ref), custom_call_target="tpu_custom_call" | custom-call | flops 100000000 | bytes 4000000 | tf_op jit(solution)/shard_map/invert/pallas_call | solution.py:38
  93.0 1.6 %copy-done.6 = bf16[4096,256]{1,0:T(8,128)(2,1)S(1)} copy-done((bf16[4096,256]{1,0:T(8,128)(2,1)S(1)}, bf16[4096,256]{1,0:T(8,128)(2,1)}, u32[]{:S(2)}) %copy-start.6) | copy-done | bytes 2097176
  94.6 3.4 %input_grad.1 = bf16[256,2048]{1,0:T(8,128)(2,1)} custom-call(s32[1]{0:T(128)} %bitcast.1.side_ref.refs_0_, bf16[256,256]{1,0:T(8,128)(2,1)} %collective-permute-done.2.grads_ref, bf16[256,256]{1,0:T(8,128)(2,1)} %collective-permute-done.3.grads_near_ref, bf16[8,512,256]{2,1,0:T(8,128)(2,1)S(1)} %bitcast.37), custom_call_target="tpu_custom_call" | custom-call | flops 1000000000 | bytes 3000000 | tf_op jit(solution)/shard_map/input_grad/pallas_call | solution.py:251
  98.0 4.3 %all-to-all-done.2.gathered_ref = bf16[16,64,128]{2,1,0:T(8,128)(2,1)S(1)} async-done(((bf16[16,64,128]{2,1,0:T(8,128)(2,1)}), bf16[16,64,128]{2,1,0:T(8,128)(2,1)S(1)}, u32[]{:S(2)}, u32[]{:S(2)}) %all-to-all-start.2) | async-done | bytes 262176 | tf_op jit(solution)/shard_map/all_to_all | solution.py:357
  102.3 0.9 finish.1
  (13 shorter events, 0.1 us)
Async XLA Ops:
  7.2 85.8 %all-gather.7.cloned.1.call-start = ((), (), s32[]{:S(2)}) async-start(), calls=%async_computation.3 | async-start | bytes 2228224 | tf_op jit(solution)/shard_map/all_gather | solution.py:305
  7.2 26.6 %copy-start = (bf16[1,1,4096,256]{3,2,1,0:T(8,128)(2,1)S(1)}, bf16[1,1,4096,256]{3,2,1,0:T(8,128)(2,1)}, u32[]{:S(2)}) copy-start(bf16[1,1,4096,256]{3,2,1,0:T(8,128)(2,1)} %param.8) | copy-start | bytes 6291460
  7.2 26.6 %copy-start.1 = (bf16[1,256,2048]{2,1,0:T(8,128)(2,1)S(1)}, bf16[1,256,2048]{2,1,0:T(8,128)(2,1)}, u32[]{:S(2)}) copy-start(bf16[1,256,2048]{2,1,0:T(8,128)(2,1)} %param.5) | copy-start | bytes 3145732
  7.2 26.6 %copy-start.5 = (f32[1,256,64]{1,2,0:T(8,128)S(1)}, f32[1,256,64]{1,2,0:T(8,128)}, u32[]{:S(2)}) copy-start(f32[1,256,64]{1,2,0:T(8,128)} %param.9) | copy-start | bytes 196612
  8.5 7.6 %collective-permute-start = (bf16[1024,256]{1,0:T(8,128)(2,1)S(1)}, bf16[1024,256]{1,0:T(8,128)(2,1)S(1)}, u32[]{:S(2)}, u32[]{:S(2)}) collective-permute-start(bf16[1024,256]{1,0:T(8,128)(2,1)S(1)} %dynamic-slice_bitcast_fusion), channel_id=1, source_target_pairs={{0,32},{32,0},{1,33},{33,1},{2,34},{34,2},{3,35},{35,3},{4,36},{36... | collective-permute-start | bytes 1572872 | tf_op jit(solution)/shard_map/ppermute | solution.py:20
  11.1 22.7 %collective-permute-start.1 = (bf16[256,256]{1,0:T(8,128)(2,1)}, bf16[256,256]{1,0:T(8,128)(2,1)}, u32[]{:S(2)}, u32[]{:S(2)}) collective-permute-start(bf16[256,256]{1,0:T(8,128)(2,1)} %bitcast.38), channel_id=1, source_target_pairs={{3,0},{451,1},{35,32},{483,33},{67,64},{387,65},{99,96},{419,97},{... | collective-permute-start | bytes 393224 | tf_op jit(solution)/shard_map/ppermute | solution.py:293
  16.1 0.8 copy-start.2
  34.5 9.2 %copy-start.4 = (bf16[1,256,256]{2,1,0:T(8,128)(2,1)S(1)}, bf16[1,256,256]{2,1,0:T(8,128)(2,1)}, u32[]{:S(2)}) copy-start(bf16[1,256,256]{2,1,0:T(8,128)(2,1)} %param.6) | copy-start | bytes 393220
  40.0 17.9 %all-to-all-start.1 = ((bf16[16,64,128]{2,1,0:T(8,128)(2,1)}), bf16[16,64,128]{2,1,0:T(8,128)(2,1)S(1)}, u32[]{:S(2)}, u32[]{:S(2)}) async-start(bf16[16,64,128]{2,1,0:T(8,128)(2,1)} %chip_sum.1), calls=%async_computation.1 | async-start | bytes 524288 | tf_op jit(solution)/shard_map/all_to_all | solution.py:322
  43.7 32.0 %collective-permute-start.2 = (bf16[256,256]{1,0:T(8,128)(2,1)S(1)}, bf16[256,256]{1,0:T(8,128)(2,1)}, u32[]{:S(2)}, u32[]{:S(2)}) collective-permute-start(bf16[256,256]{1,0:T(8,128)(2,1)S(1)} %bitcast.31), channel_id=1, source_target_pairs={{2,0},{4,2},{6,4},{8,6},{10,8},{12,10},{14,12},{16,14},{18,16},{20... | collective-permute-start | bytes 393224 | tf_op jit(solution)/shard_map/ppermute | solution.py:323
  47.3 28.4 %collective-permute-start.3 = (bf16[256,256]{1,0:T(8,128)(2,1)S(1)}, bf16[256,256]{1,0:T(8,128)(2,1)}, u32[]{:S(2)}, u32[]{:S(2)}) collective-permute-start(bf16[256,256]{1,0:T(8,128)(2,1)S(1)} %bitcast.32), channel_id=1, source_target_pairs={{3,0},{2,1},{5,2},{4,3},{7,4},{6,5},{9,6},{8,7},{11,8},{10,9},{13,... | collective-permute-start | bytes 393224 | tf_op jit(solution)/shard_map/ppermute | solution.py:324
  57.9 25.1 %copy-start.3 = (bf16[1024,256]{1,0:T(8,128)(2,1)S(1)}, bf16[1024,256]{1,0:T(8,128)(2,1)}, u32[]{:S(2)}) copy-start(bf16[1024,256]{1,0:T(8,128)(2,1)} %copy-done.2) | copy-start | bytes 1572868
  86.8 15.5 %all-to-all-start.2 = ((bf16[16,64,128]{2,1,0:T(8,128)(2,1)}), bf16[16,64,128]{2,1,0:T(8,128)(2,1)S(1)}, u32[]{:S(2)}, u32[]{:S(2)}) async-start(bf16[16,64,128]{2,1,0:T(8,128)(2,1)} %spread.1), calls=%async_computation.2 | async-start | bytes 524288 | tf_op jit(solution)/shard_map/all_to_all | solution.py:357
  93.0 1.6 %copy-start.6 = (bf16[4096,256]{1,0:T(8,128)(2,1)S(1)}, bf16[4096,256]{1,0:T(8,128)(2,1)}, u32[]{:S(2)}) copy-start(bf16[4096,256]{1,0:T(8,128)(2,1)} %all-gather.7.cloned.1.call-done) | copy-start | bytes 6291460
Sparse Core Ops, SparseCore 0:
  33.9 41.9 all-gather.6
